TPU v7x, 32 devices: a whole 2x2x4 slice. The times are simulated.
32 devices in a mesh: clip: 2 (over y), row: 16 (over z, x, core).
Axes of the slice: x: 2, y: 2, z: 4, core: 2. Of those that a mesh axis runs over, the one named last changes fastest.
Arguments:
- frames: bfloat16 [3, 48, 512], P(None, None, ('clip', 'row')), parts along dimension 2, may hold values from -1 to 1
- frame_owner: int32 [32], P('clip'), parts along dimension 0, may hold values from 0 to 15, each once
- picks: int32 [16], P('clip'), parts along dimension 0, may hold values from 0 to 15
- patch_weight: bfloat16 [768, 1024], replicated, may hold values from -0.21875 to 0.21875
- patch_bias: float32 [1024], replicated, may hold values from -6 to 6
- norm_gain: float32 [1024], replicated, may hold values from 0.1 to 1.9
- head_weight: bfloat16 [1024, 1024], replicated, may hold values from -0.1875 to 0.1875
- head_bias: float32 [1024], replicated, may hold values from -6 to 6
- head_out: float32 [1024], replicated, may hold values from -6 to 6
- hidden_state: bfloat16 [96, 16, 16, 128], P(('clip', 'row')), parts along dimension 0
- group_gain: float32 [128], replicated, may hold values from 0.1 to 1.9
- group_shift: float32 [128], replicated, may hold values from -6 to 6
- out_weight: bfloat16 [3, 3, 3, 3, 128], replicated, may hold values from -0.625 to 0.625
- inner_weight: bfloat16 [3, 3, 3, 128, 128], replicated, may hold values from -0.109375 to 0.109375
Outputs:
- inner_grad: bfloat16 [96, 16, 16, 128], P(('clip', 'row')), parts along dimension 0
There are 2 independent parts, one for each index of `clip`. A program takes and returns all parts, laid end to end along the dimension named above; an argument that names none is the same for every part. Nothing has to cross between parts.
Inputs may be any that keep to these rules, and one draw needn't show every extreme that they name: `frame_owner`: each of the 16 frames appears once.
All inputs are finite; a program needn't handle non-finite values.
Results may differ from a plain program's by a relative error of at most 0.0051.
The roundings to bfloat16 on the way count: a program that leaves them out, or rounds other values in their place, can miss the bound.
Values may be sent and summed in bfloat16 or wider, within the bound.
No kernel may reach another device: no remote copies, remote signals or barrier semaphores. Data moves between devices by JAX's collectives and lax.ppermute only.
A program may use at most 192 MiB of HBM per device.

v0:
```python
import functools

import jax
import jax.numpy as jnp
from jax import lax
from jax.experimental import pallas as pl
from jax.experimental.pallas import tpu as pltpu
from jax.sharding import PartitionSpec as P

PATCH = 16
GROUPS = 32
FRAMES = 16
LANES = 128
SLOTS = LANES // PATCH
eps_norm = 1e-06
BF16 = jnp.bfloat16
F32 = jnp.float32

SMEM = pl.BlockSpec(memory_space=pltpu.SMEM)
VMEM = pl.BlockSpec(memory_space=pltpu.VMEM)
FAR = pl.BlockSpec(memory_space=pl.ANY)


def iota(shape, dim):
    return lax.broadcasted_iota(jnp.int32, shape, dim)


def div(values, count):
    if count & (count - 1):
        return values // count
    return values >> (count.bit_length() - 1)


def mod(values, count):
    if count & (count - 1):
        return values % count
    return values & (count - 1)


def ones_where(condition):
    return jnp.where(condition, 1.0, 0.0).astype(BF16)


def matmul(left, right):
    return jnp.dot(left, right, preferred_element_type=F32)


def matmul_t(left, right):
    return lax.dot_general(left, right, (((1,), (1,)), ((), ())), preferred_element_type=F32)


def cut_in_three(values):
    high = values.astype(BF16)
    rest = values - high.astype(F32)
    middle = rest.astype(BF16)
    low = (rest - middle.astype(F32)).astype(BF16)
    return high, middle, low


def exact_rows(rows, product):
    place = iota((16, rows[0].shape[1]), 0)
    stacked = jnp.zeros(place.shape, F32)
    for index, row in enumerate(rows):
        for step, piece in enumerate(cut_in_three(row)):
            stacked = jnp.where(place == 3 * index + step, piece.astype(F32), stacked)
    result = product(stacked.astype(BF16))
    return [
        result[3 * i : 3 * i + 1] + result[3 * i + 1 : 3 * i + 2] + result[3 * i + 2 : 3 * i + 3]
        for i in range(len(rows))
    ]


def silu_slope(values):
    sigmoid = jax.nn.sigmoid(values)
    return sigmoid * (1.0 + values * (1.0 - sigmoid))


def token_rows_of(height):
    return -(-(height // PATCH) // 16) * 16


def to_tokens(pixels):
    channels, columns, height = pixels.shape
    rows = channels * columns
    token_rows = token_rows_of(height)
    flat = pixels.reshape(rows, height)
    width = channels * PATCH * columns
    lane = iota((1, width), 1)
    place = iota((rows, 1), 0)
    mine = place == div(lane, PATCH * columns) * columns + mod(lane, columns)
    in_patch = mod(div(lane, columns), PATCH)
    pixel_row = iota((height, 1), 0)
    token = iota((token_rows, 1), 0)
    tokens = jnp.zeros((token_rows, width), F32)
    for t in range(height // PATCH):
        tiled = matmul(flat, ones_where(pixel_row == in_patch + t * PATCH))
        row = jnp.sum(jnp.where(mine, tiled, 0.0), axis=0, keepdims=True)
        tokens = jnp.where(token == t, row, tokens)
    return tokens.astype(BF16)


def forward_part(tokens, count, bias, gain, load_patch):
    embedded = bias[...]
    for low, high, weight in load_patch():
        embedded = embedded + matmul(tokens[:, low:high], weight)
    centred = embedded - jnp.mean(embedded, axis=1, keepdims=True)
    inv_spread = lax.rsqrt(jnp.mean(centred * centred, axis=1, keepdims=True) + eps_norm)
    normed = centred * inv_spread
    weighted = normed * gain[...]
    inside = iota((tokens.shape[0], 1), 0) < count
    pooled = jnp.sum(jnp.where(inside, weighted, 0.0), axis=0, keepdims=True)
    return normed, inv_spread, pooled


def led_by(leader, devices):
    return [leader] + [d for d in reversed(range(devices)) if d != leader]


def first_order(devices):
    return led_by(devices * 9 // 16, devices)


def message_shape(devices):
    return jax.ShapeDtypeStruct((devices, 4, LANES), F32)


def write_windows(patch_grad, sums, own_rows, height, send):
    span = PATCH * PATCH
    line = jnp.concatenate(
        [
            jnp.concatenate([patch_grad[t : t + 1, k * span : (k + 1) * span] for t in range(height // PATCH)], axis=1)
            for k in range(3)
        ]
        + [jnp.zeros((1, height * PATCH), F32)],
        axis=0,
    )
    line = jnp.concatenate([jnp.zeros((4, LANES), F32), line, jnp.zeros((4, LANES), F32)], axis=1)
    used = iota((4, LANES), 1) < (own_rows + 4) * PATCH
    colour = iota((4, LANES), 0)
    for index, d in enumerate(first_order(send.shape[0])):
        start = LANES + (d * own_rows - 2) * PATCH
        window = jnp.where(used, line[:, start : start + LANES], 0.0)
        send[index] = jnp.where(colour < 3, window, sums[:4])


def channel_sums(hidden):
    values = hidden.reshape(-1, hidden.shape[-1]).astype(F32)
    return jnp.sum(values, axis=0, keepdims=True), jnp.sum(values * values, axis=0, keepdims=True)


def over_group(values, size):
    lane = iota(values.shape, 1)
    lanes = values.shape[1]
    step = 1
    while step < size:
        later = pltpu.roll(values, lanes - step, 1)
        earlier = pltpu.roll(values, step, 1)
        values = values + jnp.where((lane & step) == 0, later, earlier)
        step *= 2
    return values


def group_sums(hidden):
    channels = hidden.shape[-1]
    size = channels // GROUPS
    first, second = [
        over_group(jnp.broadcast_to(x, (8, channels)), size) for x in channel_sums(hidden)
    ]
    lane = mod(iota((8, channels), 1), size)
    return jnp.where(lane == 0, first, jnp.where(lane == 1, second, 0.0))


def pull_back(row, weight):
    parts = []
    for low in range(0, weight.shape[0], LANES):
        product = weight[low : low + LANES, :].astype(F32) * row
        folded = product[:, :LANES]
        for start in range(LANES, weight.shape[1], LANES):
            folded = folded + product[:, start : start + LANES]
        parts.append(jnp.sum(folded.T, axis=0, keepdims=True))
    return jnp.concatenate(parts, axis=1)


def backward_part(
    owner, picks, gain, head_bias, head_out, normed, inv_spread, pooled, weight, head, slot, own_rows, height, sums, send
):
    (before,) = exact_rows([pooled], lambda rows: matmul(rows, head[...]))
    slope = head_out[...] * silu_slope(before + head_bias[...])
    pulled = pull_back(slope, head)
    wanted = owner[slot]
    picked = jnp.int32(0)
    for k in range(picks.shape[0]):
        picked = picked + jnp.where(picks[k] == wanted, 1, 0)
    scaled = gain[...] * (picked.astype(F32) * pulled)
    token_grad = inv_spread * (
        scaled
        - jnp.mean(scaled, axis=1, keepdims=True)
        - normed * jnp.mean(scaled * normed, axis=1, keepdims=True)
    )
    patch_grad = matmul_t(token_grad.astype(BF16), weight[...]).astype(BF16).astype(F32)
    write_windows(patch_grad, sums, own_rows, height, send)


def write_edges(place, hidden, across, along):
    last = hidden.shape[0] - 1
    even = place[0] % 2 == 0
    across[0] = hidden[jnp.where(even, last, 0)]
    along[0] = hidden[jnp.where(even, 0, last)]


def reward_kernel(place, *refs):
    count, kept = 7, 4
    far, refs = refs[: count + kept + 2], refs[count + kept + 2 :]
    send, across, along = refs[:3]
    near = refs[3 + kept : 3 + kept + count] + refs[3 : 3 + kept] + refs[3 + kept + count : -1]
    sems = refs[-1]
    frames, bias, gain, owner, picks, head_bias, head_out, hidden, _, _, _, patch, head = near
    count += kept
    depth, depths = 256, (128, 256)
    small = [pltpu.make_async_copy(far[i], near[i], sems.at[i]) for i in range(count)]
    pieces = []
    used = count
    for index, rows in enumerate(depths):
        source, target = far[count + index], near[count + index]
        parts = []
        for low in range(0, target.shape[0], rows):
            part = pl.ds(low, rows)
            parts.append(pltpu.make_async_copy(source.at[part], target.at[part], sems.at[used]))
            used += 1
        pieces.append(parts)
    for copy in [small[0], small[7], small[1]] + pieces[0] + small[2:7] + pieces[1] + small[8:]:
        copy.start()

    def load_patch():
        for low in range(0, patch.shape[0], depth):
            for copy in pieces[0][low // depths[0] : (low + depth) // depths[0]]:
                copy.wait()
            yield low, low + depth, patch[low : low + depth, :]

    height = frames.shape[2]
    patches = height // PATCH
    small[0].wait()
    small[7].wait()
    tokens = to_tokens(frames[...])
    sums = group_sums(hidden[...])
    write_edges(place, hidden, across, along)
    small[1].wait()
    small[2].wait()
    normed, inv_spread, pooled = forward_part(tokens, patches, bias, gain, load_patch)
    for copy in small[3:7] + pieces[1]:
        copy.wait()
    backward_part(
        owner,
        picks,
        gain,
        head_bias,
        head_out,
        normed,
        inv_spread,
        pooled / patches,
        patch,
        head,
        place[0],
        hidden.shape[0],
        height,
        sums,
        send,
    )
    for copy in small[8:]:
        copy.wait()


def forward_kernel(frames, bias, gain, patch, normed, inv_spread, pooled):
    width = patch.shape[0]
    tokens = to_tokens(frames[...])
    normed[...], spread, pooled[...] = forward_part(
        tokens, frames.shape[2] // PATCH, bias, gain, lambda: [(0, width, patch[...])]
    )
    inv_spread[...] = jnp.broadcast_to(spread, inv_spread.shape)


def backward_kernel(
    owner,
    picks,
    place,
    hidden,
    gain,
    head_bias,
    head_out,
    normed,
    inv_spread,
    pooled,
    patch,
    head,
    send,
    across,
    along,
    *,
    height,
    per_frame,
):
    write_edges(place, hidden, across, along)
    backward_part(
        owner,
        picks,
        gain,
        head_bias,
        head_out,
        normed[...],
        inv_spread[...][:, :1],
        pooled[...],
        patch,
        head,
        place[0] // per_frame,
        hidden.shape[0],
        height,
        group_sums(hidden[...]),
        send,
    )


def params(cells):
    return pltpu.CompilerParams(vmem_limit_bytes=min(16 + cells // 64, 48) * 1024 * 1024)


def near(array):
    return pltpu.with_memory_space_constraint(array, pltpu.VMEM)


def far(array):
    return pltpu.with_memory_space_constraint(array, pltpu.HBM)


def prepare_kernel(out_weight, wide, scratch):
    block = scratch.shape[0] // 3
    amount = scratch.shape[1] // LANES
    span = 3 * (amount + 2)
    scratch[...] = jnp.zeros_like(scratch)
    for a in range(3):
        for e in range(3):
            for b in range(3):
                piece = out_weight[a, b, e].astype(F32)
                for i in range(amount):
                    start = a * block + e * span + 3 * (i - b + 2)
                    scratch[start : start + 3, i * LANES : (i + 1) * LANES] = piece
    wide[...] = scratch[...].astype(BF16)


def norm_constants(totals, cell_total):
    channels = totals.shape[1]
    size = channels // GROUPS
    totals = jnp.broadcast_to(totals, (8, channels))
    lane = mod(iota((8, channels), 1), size)
    first, second = [over_group(jnp.where(lane == i, totals, 0.0), size)[:1] for i in range(2)]
    mean = first / cell_total
    return mean, lax.rsqrt(second / cell_total - mean * mean + eps_norm)


def norm_slopes(state, mean, inverse, gain, shift):
    normed = (state - mean) * inverse
    return normed, silu_slope(normed * gain + shift) * gain


def slope_kernel(
    owner, arrived, hidden, gain, shift, wide, direct, edge_slopes, stats, sums, slopes_own, received
):
    devices, message_rows, _ = arrived.shape
    own_rows, frame_count, width, channels = hidden.shape
    cells = frame_count * width
    per_frame = devices // frame_count
    received[...] = arrived[...].reshape(received.shape)

    def from_all(row):
        return received[pl.ds(row, devices, stride=message_rows), :]

    totals = jnp.sum(from_all(3), axis=0, keepdims=True)
    mean, inverse = norm_constants(totals, own_rows * devices * cells * (channels // GROUPS))
    for i in range(own_rows):
        state = hidden[i].reshape(cells, channels).astype(F32)
        slopes_own[i] = norm_slopes(state, mean, inverse, gain[...], shift[...])[1]

    lines = jnp.concatenate([from_all(k) for k in range(3)], axis=1).astype(BF16)
    place = iota((1, devices), 1)
    source = jnp.zeros_like(place)
    for index, d in enumerate(first_order(devices)):
        source = jnp.where(place == index, d, source)
    home = jnp.zeros((1, devices), jnp.int32)
    for b in range(frame_count):
        home = jnp.where(div(source, per_frame) == b, owner[b] * per_frame, home)
    home = home + mod(source, per_frame)
    cell = iota((cells, 1), 0)
    column = mod(cell, width)
    frame_strip = div(cell, width) * per_frame
    lane = mod(iota((1, 3 * LANES), 1), PATCH)
    kept = []
    placed = None
    for e in range(3):
        wanted = column - e + 1
        if per_frame > 1 or placed is None:
            strip = frame_strip + div(wanted, PATCH) if per_frame > 1 else frame_strip
            placed = matmul(ones_where(home == strip), lines)
        inside = jnp.where((wanted >= 0) & (wanted < width), mod(wanted, PATCH), -1)
        kept.append(jnp.where(lane == inside, placed, 0.0).astype(BF16))
    block = wide.shape[0] // 3
    span = 3 * (own_rows + 4)
    entry = iota((3 * LANES, 1), 0)
    entry = div(mod(entry, LANES), PATCH) * 3 + div(entry, LANES)
    entry = jnp.where(entry < span, entry, -3 * span)
    tap = iota((1, block), 1)
    folds = jnp.concatenate([ones_where(tap == entry + e * span) for e in range(3)], axis=0)
    taps = matmul(jnp.concatenate(kept, axis=1), folds).astype(BF16)
    later = []
    for a in range(3):
        skip = (2 - a) * width
        later.append(
            jnp.concatenate([taps[skip:], jnp.zeros((skip, block), BF16)], axis=0) if skip else taps
        )
    result = matmul(jnp.concatenate(later, axis=1), wide[...])

    first = jnp.zeros((1, channels), F32)
    second = jnp.zeros((1, channels), F32)
    for i in range(own_rows):
        state = hidden[i].reshape(cells, channels).astype(F32)
        up = result[:, (i + 1) * channels : (i + 2) * channels] * slopes_own[i]
        direct[i] = up * inverse
        first = first + jnp.sum(up, axis=0, keepdims=True)
        second = second + jnp.sum(up * ((state - mean) * inverse), axis=0, keepdims=True)
    edge_slopes[0] = result[:, :channels]
    edge_slopes[1] = result[:, (own_rows + 1) * channels :]
    stats[0:1, :] = mean
    stats[1:2, :] = inverse
    both = jnp.where(iota((2, channels), 0) == 0, first, second)
    sums[...] = jnp.broadcast_to(both[None], sums.shape)


def late_kernel(
    place, across, along, slopes, stats, gain, shift, far_weight, direct, states, turned, inner_weight, sem
):
    copy = pltpu.make_async_copy(far_weight, inner_weight, sem.at[0])
    copy.start()
    cells, channels = slopes.shape[1:]
    odd = place[0] % 2 == 1
    mean = stats[0:1, :]
    inverse = stats[1:2, :]
    for i in range(2):
        state = jnp.where(odd == (i == 0), across[0], along[0])
        states[i] = state
        values = state.reshape(cells, channels).astype(F32)
        direct[i] = slopes[i] * norm_slopes(values, mean, inverse, gain[...], shift[...])[1] * inverse
    copy.wait()
    size = inner_weight.shape[3]
    for b in range(3):
        for a in range(3):
            for e in range(3):
                at = (a * 3 + e) * size
                turned[at : at + size, b * size : (b + 1) * size] = inner_weight[a, b, e].T


def inner_kernel(
    place, arrived, stats, direct, hidden, edge_direct, edge_states, turned, far_out, padded, out, sems, *, devices
):
    own_rows, frame_count, width, channels = out.shape
    cells = frame_count * width
    totals = jnp.sum(arrived[...], axis=0)
    cell_total = own_rows * devices * cells * (channels // GROUPS)
    place_row = iota((8, channels), 0)
    both = jnp.where(place_row == 0, totals[0:1], totals[1:2])
    both = over_group(both, channels // GROUPS)
    first, second = both[0:1], both[1:2]
    mean = stats[0:1, :]
    inverse = stats[1:2, :]
    constant = first / cell_total * inverse
    factor = second / cell_total * inverse * inverse
    position = place[0]
    in_frame = mod(iota((cells, 1), 0), width)
    for i in range(own_rows + 2):
        if 0 < i < own_rows + 1:
            state, part = hidden[i - 1], direct[i - 1]
        else:
            state, part = edge_states[min(i, 1)], edge_direct[min(i, 1)]
        grad = part - constant - (state.reshape(cells, channels).astype(F32) - mean) * factor
        if i == 0:
            grad = jnp.where(position > 0, grad, 0.0)
        if i == own_rows + 1:
            grad = jnp.where(position < devices - 1, grad, 0.0)
        after = jnp.where(in_frame < width - 1, pltpu.roll(grad, cells - 1, 0), 0.0)
        prior = jnp.where(in_frame > 0, pltpu.roll(grad, 1, 0), 0.0)
        padded[i, :cells, 0:channels] = after.astype(BF16)
        padded[i, :cells, channels : 2 * channels] = grad.astype(BF16)
        padded[i, :cells, 2 * channels :] = prior.astype(BF16)
        padded[i, cells:, :] = jnp.zeros((2 * width, 3 * channels), BF16)
    results = [jnp.zeros((cells, channels), F32) for _ in range(own_rows)]
    copies = []
    for i in range(own_rows + 2):
        joined = jnp.concatenate(
            [padded[i, (2 - a) * width : (2 - a) * width + cells, :] for a in range(3)], axis=1
        )
        taps = [b for b in range(3) if 0 <= i + b - 2 < own_rows]
        for low in range(0, len(taps), 2):
            some = taps[low : low + 2]
            product = matmul(joined, turned[:, some[0] * channels : (some[-1] + 1) * channels])
            for step, b in enumerate(some):
                results[i + b - 2] = results[i + b - 2] + product[:, step * channels : (step + 1) * channels]
        if i >= 2:
            out[i - 2] = results[i - 2].reshape(frame_count, width, channels).astype(BF16)
            copies.append(pltpu.make_async_copy(out.at[i - 2], far_out.at[i - 2], sems.at[i - 2]))
            copies[-1].start()
    for copy in copies:
        copy.wait()


def per_device(
    frames,
    frame_owner,
    picks,
    patch_weight,
    patch_bias,
    norm_gain,
    head_weight,
    head_bias,
    head_out,
    hidden_state,
    group_gain,
    group_shift,
    out_weight,
    inner_weight,
):
    devices = lax.axis_size("row")
    position = lax.axis_index("row").astype(jnp.int32).reshape(1)
    per_frame = devices // FRAMES
    height = frames.shape[1]
    own_rows, _, frame_width, channels = hidden_state.shape
    cells = FRAMES * frame_width
    width = patch_weight.shape[1]
    turned_frames = jnp.transpose(frames, (0, 2, 1))
    bias = patch_bias.reshape(1, width)
    gain = norm_gain.reshape(1, width)
    head_bias_row = head_bias.reshape(1, width)
    head_out_row = head_out.reshape(1, width)
    state_rows = own_rows + 2
    tap_rows = -(-9 * (own_rows + 4) // LANES) * LANES
    edge = jax.ShapeDtypeStruct((1,) + hidden_state.shape[1:], BF16)
    message = (message_shape(devices), edge, edge)
    gain_row = group_gain.reshape(1, channels)
    shift_row = group_shift.reshape(1, channels)
    early = [hidden_state, gain_row, shift_row, out_weight]
    slope_outs = (
        pltpu.VMEM((own_rows, cells, channels), F32),
        pltpu.VMEM((2, cells, channels), F32),
        pltpu.VMEM((8, channels), F32),
        jax.ShapeDtypeStruct((devices, 2, channels), F32),
    )
    if per_frame == 1:
        arrays = [turned_frames, bias, gain, frame_owner, picks, head_bias_row, head_out_row]
        weights = [patch_weight, head_weight]

        def scratch(x):
            return (pltpu.SMEM if x.dtype == jnp.int32 else pltpu.VMEM)(x.shape, x.dtype)

        send, across, along, *early = pl.pallas_call(
            reward_kernel,
            out_shape=message + tuple(pltpu.VMEM(x.shape, x.dtype) for x in early),
            in_specs=[SMEM] + [FAR] * (len(arrays) + len(early) + len(weights)),
            out_specs=[VMEM] * (3 + len(early)),
            scratch_shapes=[scratch(x) for x in arrays + weights] + [pltpu.SemaphoreType.DMA((32,))],
            compiler_params=params(0),
            name="reward",
        )(position, *[far(x) for x in arrays + early + weights])
    else:
        count = height // PATCH
        normed, inv_spread, partial = pl.pallas_call(
            forward_kernel,
            out_shape=(
                jax.ShapeDtypeStruct((token_rows_of(height), width), F32),
                jax.ShapeDtypeStruct((token_rows_of(height), LANES), F32),
                jax.ShapeDtypeStruct((1, width), F32),
            ),
            compiler_params=params(cells),
            name="reward_forward",
        )(turned_frames, bias, gain, patch_weight)
        members = [[b * per_frame + i for i in range(per_frame)] for b in range(FRAMES)]
        pooled = lax.psum(partial, "row", axis_index_groups=members) / (count * per_frame)
        send, across, along = pl.pallas_call(
            functools.partial(backward_kernel, height=height, per_frame=per_frame),
            out_shape=message,
            in_specs=[SMEM] * 3 + [VMEM] * 9,
            out_specs=[VMEM] * 3,
            compiler_params=params(cells),
            name="reward_backward",
        )(
            frame_owner,
            picks,
            position,
            hidden_state,
            gain,
            head_bias_row,
            head_out_row,
            normed,
            inv_spread,
            pooled,
            patch_weight,
            head_weight,
        )
    early = [near(x) for x in early]
    wide = pl.pallas_call(
        prepare_kernel,
        out_shape=pltpu.VMEM((3 * tap_rows, state_rows * channels), BF16),
        in_specs=[VMEM],
        scratch_shapes=[pltpu.VMEM((3 * tap_rows, state_rows * channels), F32)],
        compiler_params=params(cells),
        name="prepare",
    )(early[3])
    arrived = lax.all_to_all(send, "row", 0, 0, axis_index_groups=[first_order(devices)], tiled=True)
    direct, edge_slopes, stats, sums = pl.pallas_call(
        slope_kernel,
        out_shape=slope_outs,
        in_specs=[SMEM] + [VMEM] * 5,
        scratch_shapes=[
            pltpu.VMEM((own_rows, cells, channels), F32),
            pltpu.VMEM((4 * devices, LANES), F32),
        ],
        compiler_params=params(cells),
        name="slope",
    )(frame_owner, near(arrived), *early[:3], near(wide))
    swaps = [(2 * i, 2 * i + 1) for i in range(devices // 2)]
    across = lax.ppermute(across, "row", swaps + [(b, a) for a, b in swaps])
    swaps = [(2 * i - 1, 2 * i) for i in range(1, devices // 2)]
    along = lax.ppermute(along, "row", swaps + [(b, a) for a, b in swaps])
    summed = lax.all_to_all(sums, "row", 0, 0, axis_index_groups=[led_by(devices - 1, devices)], tiled=True)
    edge_direct, edge_states, turned = pl.pallas_call(
        late_kernel,
        out_shape=(
            pltpu.VMEM((2, cells, channels), F32),
            pltpu.VMEM((2,) + hidden_state.shape[1:], BF16),
            pltpu.VMEM((9 * channels, 3 * channels), BF16),
        ),
        in_specs=[SMEM] + [VMEM] * 6 + [FAR],
        scratch_shapes=[pltpu.VMEM(inner_weight.shape, BF16), pltpu.SemaphoreType.DMA((1,))],
        input_output_aliases={3: 0},
        compiler_params=params(cells),
        name="late",
    )(position, near(across), near(along), near(edge_slopes), near(stats), *early[1:3], far(inner_weight))
    return pl.pallas_call(
        functools.partial(inner_kernel, devices=devices),
        out_shape=jax.ShapeDtypeStruct(hidden_state.shape, BF16),
        in_specs=[SMEM] + [VMEM] * 7,
        out_specs=FAR,
        scratch_shapes=[
            pltpu.VMEM((own_rows + 2, cells + 2 * frame_width, 3 * channels), BF16),
            pltpu.VMEM(hidden_state.shape, BF16),
            pltpu.SemaphoreType.DMA((own_rows,)),
        ],
        compiler_params=params(cells),
        name="inner",
    )(
        position,
        near(summed),
        near(stats),
        near(direct),
        early[0],
        near(edge_direct),
        near(edge_states),
        near(turned),
    )


def solution(mesh):
    return jax.shard_map(
        per_device,
        mesh=mesh,
        in_specs=(
            P(None, None, ("clip", "row")),
            P("clip"),
            P("clip"),
            P(),
            P(),
            P(),
            P(),
            P(),
            P(),
            P(("clip", "row"), None, None, None),
            P(),
            P(),
            P(),
            P(),
        ),
        out_specs=P(("clip", "row"), None, None, None),
        check_vma=False,
    )
```

profile of v0, /device:TPU:0, one launch (start us, length us, event | category | flops | bytes accessed | tf_op | source)
XLA Modules:
  0.0 28.6 jit_solution(7213151814983457066)
XLA Ops:
  0.0 0.0 copy-start
  0.0 4.5 %reward.1 = (f32[16,4,128]{2,1,0:T(4,128)}, bf16[1,16,16,128]{3,2,1,0:T(8,128)(2,1)S(1)}, bf16[1,16,16,128]{3,2,1,0:T(8,128)(2,1)S(1)}, bf16[3,16,16,128]{3,2,1,...) custom-call(s32[1]{0:T(128)} %bitcast.place, ...), custom_call_target="tpu_custom_call" | custom-call | tf_op jit(solution)/shard_map/reward/pallas_call | solution.py:560
  4.5 7.6 %all-to-all-start = ((f32[16,4,128]{2,1,0:T(4,128)}), f32[16,4,128]{2,1,0:T(4,128)S(1)}, u32[]{:S(2)}, u32[]{:S(2)}) async-start(f32[16,4,128]{2,1,0:T(4,128)} %get-tuple-element.19), calls=%async_computation | async-start | bytes 65536 | tf_op jit(solution)/shard_map/all_to_all | solution.py:613
  12.1 0.1 collective-permute-start
  12.2 0.7 %collective-permute-start.1 = (bf16[1,16,16,128]{3,2,1,0:T(8,128)(2,1)S(1)}, bf16[1,16,16,128]{3,2,1,0:T(8,128)(2,1)S(1)}, u32[]{:S(2)}, u32[]{:S(2)}) collective-permute-start(bf16[1,16,16,128]{3,2,1,0:T(8,128)(2,1)S(1)} %get-tuple-element.28), channel_id=1, source_target_pairs={{1,2},{3,4},{5,6},{7,8},{9,10},{11,12},{13,14},{2,1},{4,3},{6,5},{... | collective-permute-start | bytes 196616 | tf_op jit(solution)/shard_map/ppermute | solution.py:628
  12.9 0.1 prepare.1.wide
  13.0 3.5 %all-to-all-done.arrived = f32[16,4,128]{2,1,0:T(4,128)S(1)} async-done(((f32[16,4,128]{2,1,0:T(4,128)}), f32[16,4,128]{2,1,0:T(4,128)S(1)}, u32[]{:S(2)}, u32[]{:S(2)}) %all-to-all-start) | async-done | bytes 32800 | tf_op jit(solution)/shard_map/all_to_all | solution.py:613
  16.5 0.0 copy-done
  16.5 1.9 %slope.1 = (f32[3,256,128]{2,1,0:T(8,128)S(1)}, f32[2,256,128]{2,1,0:T(8,128)S(1)}, f32[8,128]{1,0:T(8,128)S(1)}, f32[16,2,128]{2,1,0:T(2,128)}) custom-call(s32[16]{0:T(128)S(1)} %copy-done, f32[16,4,128]{2,1,0:T(4,128)S(1)} %all-to-all-done.arrived, bf16[3,16,16,128]{3,2,1,0:T(8,128)(2,1)S(1)} %get-tuple-element.20.hidden, ...), custom_call_target="tpu_custom_call" | custom-call | tf_op jit(solution)/shard_map/slope/pallas_call | solution.py:614
  18.5 5.8 %all-to-all-start.1 = ((f32[16,2,128]{2,1,0:T(2,128)}), f32[16,2,128]{2,1,0:T(2,128)S(1)}, u32[]{:S(2)}, u32[]{:S(2)}) async-start(f32[16,2,128]{2,1,0:T(2,128)} %get-tuple-element.24), calls=%async_computation.1 | async-start | bytes 32768 | tf_op jit(solution)/shard_map/all_to_all | solution.py:629
  24.2 0.0 collective-permute-done.across
  24.2 0.0 collective-permute-done.1.along
  24.2 1.5 %late.1 = (f32[2,256,128]{2,1,0:T(8,128)S(1)}, bf16[2,16,16,128]{3,2,1,0:T(8,128)(2,1)S(1)}, bf16[1152,384]{1,0:T(8,128)(2,1)S(1)}) custom-call(s32[1]{0:T(128)} %bitcast.place, bf16[1,16,16,128]{3,2,1,0:T(8,128)(2,1)S(1)} %collective-permute-done.across, bf16[1,16,16,128]{3,2,1,0:T(8,128)(2,1)S(1)} %collective-permute-done.1.along, ...), custom_call_target="tpu_custom_call", output_to_operand_aliasing={{0}: (3, {})} | custom-call | tf_op jit(solution)/shard_map/late/pallas_call | solution.py:630
  25.7 0.9 %all-to-all-done.1.arrived = f32[16,2,128]{2,1,0:T(2,128)S(1)} async-done(((f32[16,2,128]{2,1,0:T(2,128)}), f32[16,2,128]{2,1,0:T(2,128)S(1)}, u32[]{:S(2)}, u32[]{:S(2)}) %all-to-all-start.1) | async-done | bytes 16416 | tf_op jit(solution)/shard_map/all_to_all | solution.py:629
  26.6 2.0 %inner.1 = bf16[3,16,16,128]{3,2,1,0:T(8,128)(2,1)} custom-call(s32[1]{0:T(128)} %bitcast.place, f32[16,2,128]{2,1,0:T(2,128)S(1)} %all-to-all-done.1.arrived, f32[8,128]{1,0:T(8,128)S(1)} %get-tuple-element.25.stats, f32[3,256,128]{2,1,0:T(8,128)S(1)} %get-tuple-element.26.direct, bf16[3,16,16,128]{3,2,1,0:T(8,128)(2,1)S(1)} %get-tuple-element.20.hidden, ...), custom_call_target="tpu_custom_call" | custom-call | tf_op jit(solution)/shard_map/inner/pallas_call | solution.py:643
Async XLA Ops:
  0.0 16.5 %copy-start = (s32[16]{0:T(128)S(1)}, s32[16]{0:T(128)}, u32[]{:S(2)}) copy-start(s32[16]{0:T(128)} %owner.1) | copy-start | bytes 196
  4.5 12.0 %all-to-all-start = ((f32[16,4,128]{2,1,0:T(4,128)}), f32[16,4,128]{2,1,0:T(4,128)S(1)}, u32[]{:S(2)}, u32[]{:S(2)}) async-start(f32[16,4,128]{2,1,0:T(4,128)} %get-tuple-element.19), calls=%async_computation | async-start | bytes 65536 | tf_op jit(solution)/shard_map/all_to_all | solution.py:613
  12.1 12.1 %collective-permute-start = (bf16[1,16,16,128]{3,2,1,0:T(8,128)(2,1)S(1)}, bf16[1,16,16,128]{3,2,1,0:T(8,128)(2,1)S(1)}, u32[]{:S(2)}, u32[]{:S(2)}) collective-permute-start(bf16[1,16,16,128]{3,2,1,0:T(8,128)(2,1)S(1)} %get-tuple-element.27), channel_id=1, source_target_pairs={{0,1},{2,3},{4,5},{6,7},{8,9},{10,11},{12,13},{14,15},{1,0},{3,2},... | collective-permute-start | bytes 196616 | tf_op jit(solution)/shard_map/ppermute | solution.py:626
  12.2 12.0 %collective-permute-start.1 = (bf16[1,16,16,128]{3,2,1,0:T(8,128)(2,1)S(1)}, bf16[1,16,16,128]{3,2,1,0:T(8,128)(2,1)S(1)}, u32[]{:S(2)}, u32[]{:S(2)}) collective-permute-start(bf16[1,16,16,128]{3,2,1,0:T(8,128)(2,1)S(1)} %get-tuple-element.28), channel_id=1, source_target_pairs={{1,2},{3,4},{5,6},{7,8},{9,10},{11,12},{13,14},{2,1},{4,3},{6,5},{... | collective-permute-start | bytes 196616 | tf_op jit(solution)/shard_map/ppermute | solution.py:628
  18.5 8.2 %all-to-all-start.1 = ((f32[16,2,128]{2,1,0:T(2,128)}), f32[16,2,128]{2,1,0:T(2,128)S(1)}, u32[]{:S(2)}, u32[]{:S(2)}) async-start(f32[16,2,128]{2,1,0:T(2,128)} %get-tuple-element.24), calls=%async_computation.1 | async-start | bytes 32768 | tf_op jit(solution)/shard_map/all_to_all | solution.py:629
where the time goes:
time: 28.9 us; the launch traced here: 28.6 us
  starting transfers between devices  14.1 us (49%)
  Pallas kernels  10.1 us (35%)
  waiting for transfers between devices  4.4 us (15%)
    all_to_all x1, starting transfers between devices, per_device(): lax.all_to_all(send, 'row', 0, 0, axis_index_groups=[first_order(devices)...  7.6 us
    all_to_all x1, starting transfers between devices, per_device(): lax.all_to_all(sums, 'row', 0, 0, axis_index_groups=[led_by(devices - 1,...  5.77 us
    pallas_call x1, Pallas kernels, per_device(): pl.pallas_call(reward_kernel, out_shape=message + tuple((pltpu.VMEM(x.sha...  4.53 us
    all_to_all x1, waiting for transfers between devices, per_device(): lax.all_to_all(send, 'row', 0, 0, axis_index_groups=[first_order(devices)...  3.5 us
    pallas_call x1, Pallas kernels, per_device(): pl.pallas_call(functools.partial(inner_kernel, devices=devices), out_shap...  2.02 us
    pallas_call x1, Pallas kernels, per_device(): pl.pallas_call(slope_kernel, out_shape=slope_outs, in_specs=[SMEM] + [VME...  1.95 us
    pallas_call x1, Pallas kernels, per_device(): pl.pallas_call(late_kernel, out_shape=(pltpu.VMEM((2, cells, channels), F...  1.47 us
    all_to_all x1, waiting for transfers between devices, per_device(): lax.all_to_all(sums, 'row', 0, 0, axis_index_groups=[led_by(devices - 1,...  0.89 us
  transfers between devices with their start and end apart: 4, of which 2 were waited for; matrix products, arithmetic and copies ran while one was open for 0% of the time, Pallas kernels for 12%

commit v1 on v0

--- a/solution.py
+++ b/solution.py
@@ -182,9 +182,9 @@
 
 
 def backward_part(
-    owner, picks, gain, head_bias, head_out, normed, inv_spread, pooled, weight, head, slot, own_rows, height, sums, send
+    owner, picks, gain, head_bias, head_out, normed, inv_spread, pooled, weight, head, through_head, slot, own_rows, height, sums, send
 ):
-    (before,) = exact_rows([pooled], lambda rows: matmul(rows, head[...]))
+    (before,) = exact_rows([pooled], through_head)
     slope = head_out[...] * silu_slope(before + head_bias[...])
     pulled = pull_back(slope, head)
     wanted = owner[slot]
@@ -247,8 +247,16 @@
     small[1].wait()
     small[2].wait()
     normed, inv_spread, pooled = forward_part(tokens, patches, bias, gain, load_patch)
-    for copy in small[3:7] + pieces[1]:
+    for copy in small[3:7]:
         copy.wait()
+
+    def through_head(rows):
+        total = jnp.zeros((rows.shape[0], head.shape[1]), F32)
+        for index, low in enumerate(range(0, head.shape[0], depths[1])):
+            pieces[1][index].wait()
+            total = total + matmul(rows[:, low : low + depths[1]], head[low : low + depths[1], :])
+        return total
+
     backward_part(
         owner,
         picks,
@@ -260,6 +268,7 @@
         pooled / patches,
         patch,
         head,
+        through_head,
         place[0],
         hidden.shape[0],
         height,
@@ -311,6 +320,7 @@
         pooled[...],
         patch,
         head,
+        lambda rows: matmul(rows, head[...]),
         place[0] // per_frame,
         hidden.shape[0],
         height,

time: 28.9 us -> 28.7 us (level)
  no operation moved by 1% of the time
where the time goes in v1:
time: 28.7 us; the launch traced here: 28.4 us
  starting transfers between devices  14.1 us (49%)
  Pallas kernels  9.89 us (34%)
  waiting for transfers between devices  4.4 us (15%)
    all_to_all x1, starting transfers between devices, per_device(): lax.all_to_all(send, 'row', 0, 0, axis_index_groups=[first_order(devices)...  7.6 us
    all_to_all x1, starting transfers between devices, per_device(): lax.all_to_all(sums, 'row', 0, 0, axis_index_groups=[led_by(devices - 1,...  5.77 us
    pallas_call x1, Pallas kernels, per_device(): pl.pallas_call(reward_kernel, out_shape=message + tuple((pltpu.VMEM(x.sha...  4.34 us
    all_to_all x1, waiting for transfers between devices, per_device(): lax.all_to_all(send, 'row', 0, 0, axis_index_groups=[first_order(devices)...  3.5 us
    pallas_call x1, Pallas kernels, per_device(): pl.pallas_call(functools.partial(inner_kernel, devices=devices), out_shap...  2.02 us
    pallas_call x1, Pallas kernels, per_device(): pl.pallas_call(slope_kernel, out_shape=slope_outs, in_specs=[SMEM] + [VME...  1.95 us
    pallas_call x1, Pallas kernels, per_device(): pl.pallas_call(late_kernel, out_shape=(pltpu.VMEM((2, cells, channels), F...  1.47 us
    all_to_all x1, waiting for transfers between devices, per_device(): lax.all_to_all(sums, 'row', 0, 0, axis_index_groups=[led_by(devices - 1,...  0.89 us
  transfers between devices with their start and end apart: 4, of which 2 were waited for; matrix products, arithmetic and copies ran while one was open for 0% of the time, Pallas kernels for 12%

profile of v1, /device:TPU:0, one launch (start us, length us, event | category | flops | bytes accessed | tf_op | source)
XLA Modules:
  0.0 28.4 jit_solution(3488464815633907435)
XLA Ops:
  0.0 0.0 copy-start
  0.0 4.3 %reward.1 = (f32[16,4,128]{2,1,0:T(4,128)}, bf16[1,16,16,128]{3,2,1,0:T(8,128)(2,1)S(1)}, bf16[1,16,16,128]{3,2,1,0:T(8,128)(2,1)S(1)}, bf16[3,16,16,128]{3,2,1,...) custom-call(s32[1]{0:T(128)} %bitcast.place, ...), custom_call_target="tpu_custom_call" | custom-call | tf_op jit(solution)/shard_map/reward/pallas_call | solution.py:570
  4.3 7.6 %all-to-all-start = ((f32[16,4,128]{2,1,0:T(4,128)}), f32[16,4,128]{2,1,0:T(4,128)S(1)}, u32[]{:S(2)}, u32[]{:S(2)}) async-start(f32[16,4,128]{2,1,0:T(4,128)} %get-tuple-element.19), calls=%async_computation | async-start | bytes 65536 | tf_op jit(solution)/shard_map/all_to_all | solution.py:623
  12.0 0.1 collective-permute-start
  12.0 0.7 %collective-permute-start.1 = (bf16[1,16,16,128]{3,2,1,0:T(8,128)(2,1)S(1)}, bf16[1,16,16,128]{3,2,1,0:T(8,128)(2,1)S(1)}, u32[]{:S(2)}, u32[]{:S(2)}) collective-permute-start(bf16[1,16,16,128]{3,2,1,0:T(8,128)(2,1)S(1)} %get-tuple-element.28), channel_id=1, source_target_pairs={{1,2},{3,4},{5,6},{7,8},{9,10},{11,12},{13,14},{2,1},{4,3},{6,5},{... | collective-permute-start | bytes 196616 | tf_op jit(solution)/shard_map/ppermute | solution.py:638
  12.7 0.1 prepare.1.wide
  12.8 3.5 %all-to-all-done.arrived = f32[16,4,128]{2,1,0:T(4,128)S(1)} async-done(((f32[16,4,128]{2,1,0:T(4,128)}), f32[16,4,128]{2,1,0:T(4,128)S(1)}, u32[]{:S(2)}, u32[]{:S(2)}) %all-to-all-start) | async-done | bytes 32800 | tf_op jit(solution)/shard_map/all_to_all | solution.py:623
  16.3 0.0 copy-done
  16.3 1.9 %slope.1 = (f32[3,256,128]{2,1,0:T(8,128)S(1)}, f32[2,256,128]{2,1,0:T(8,128)S(1)}, f32[8,128]{1,0:T(8,128)S(1)}, f32[16,2,128]{2,1,0:T(2,128)}) custom-call(s32[16]{0:T(128)S(1)} %copy-done, f32[16,4,128]{2,1,0:T(4,128)S(1)} %all-to-all-done.arrived, bf16[3,16,16,128]{3,2,1,0:T(8,128)(2,1)S(1)} %get-tuple-element.20.hidden, ...), custom_call_target="tpu_custom_call" | custom-call | tf_op jit(solution)/shard_map/slope/pallas_call | solution.py:624
  18.3 5.8 %all-to-all-start.1 = ((f32[16,2,128]{2,1,0:T(2,128)}), f32[16,2,128]{2,1,0:T(2,128)S(1)}, u32[]{:S(2)}, u32[]{:S(2)}) async-start(f32[16,2,128]{2,1,0:T(2,128)} %get-tuple-element.24), calls=%async_computation.1 | async-start | bytes 32768 | tf_op jit(solution)/shard_map/all_to_all | solution.py:639
  24.0 0.0 collective-permute-done.across
  24.0 0.0 collective-permute-done.1.along
  24.0 1.5 %late.1 = (f32[2,256,128]{2,1,0:T(8,128)S(1)}, bf16[2,16,16,128]{3,2,1,0:T(8,128)(2,1)S(1)}, bf16[1152,384]{1,0:T(8,128)(2,1)S(1)}) custom-call(s32[1]{0:T(128)} %bitcast.place, bf16[1,16,16,128]{3,2,1,0:T(8,128)(2,1)S(1)} %collective-permute-done.across, bf16[1,16,16,128]{3,2,1,0:T(8,128)(2,1)S(1)} %collective-permute-done.1.along, ...), custom_call_target="tpu_custom_call", output_to_operand_aliasing={{0}: (3, {})} | custom-call | tf_op jit(solution)/shard_map/late/pallas_call | solution.py:640
  25.5 0.9 %all-to-all-done.1.arrived = f32[16,2,128]{2,1,0:T(2,128)S(1)} async-done(((f32[16,2,128]{2,1,0:T(2,128)}), f32[16,2,128]{2,1,0:T(2,128)S(1)}, u32[]{:S(2)}, u32[]{:S(2)}) %all-to-all-start.1) | async-done | bytes 16416 | tf_op jit(solution)/shard_map/all_to_all | solution.py:639
  26.4 2.0 %inner.1 = bf16[3,16,16,128]{3,2,1,0:T(8,128)(2,1)} custom-call(s32[1]{0:T(128)} %bitcast.place, f32[16,2,128]{2,1,0:T(2,128)S(1)} %all-to-all-done.1.arrived, f32[8,128]{1,0:T(8,128)S(1)} %get-tuple-element.25.stats, f32[3,256,128]{2,1,0:T(8,128)S(1)} %get-tuple-element.26.direct, bf16[3,16,16,128]{3,2,1,0:T(8,128)(2,1)S(1)} %get-tuple-element.20.hidden, ...), custom_call_target="tpu_custom_call" | custom-call | tf_op jit(solution)/shard_map/inner/pallas_call | solution.py:653
Async XLA Ops:
  0.0 16.3 %copy-start = (s32[16]{0:T(128)S(1)}, s32[16]{0:T(128)}, u32[]{:S(2)}) copy-start(s32[16]{0:T(128)} %owner.1) | copy-start | bytes 196
  4.3 12.0 %all-to-all-start = ((f32[16,4,128]{2,1,0:T(4,128)}), f32[16,4,128]{2,1,0:T(4,128)S(1)}, u32[]{:S(2)}, u32[]{:S(2)}) async-start(f32[16,4,128]{2,1,0:T(4,128)} %get-tuple-element.19), calls=%async_computation | async-start | bytes 65536 | tf_op jit(solution)/shard_map/all_to_all | solution.py:623
  12.0 12.1 %collective-permute-start = (bf16[1,16,16,128]{3,2,1,0:T(8,128)(2,1)S(1)}, bf16[1,16,16,128]{3,2,1,0:T(8,128)(2,1)S(1)}, u32[]{:S(2)}, u32[]{:S(2)}) collective-permute-start(bf16[1,16,16,128]{3,2,1,0:T(8,128)(2,1)S(1)} %get-tuple-element.27), channel_id=1, source_target_pairs={{0,1},{2,3},{4,5},{6,7},{8,9},{10,11},{12,13},{14,15},{1,0},{3,2},... | collective-permute-start | bytes 196616 | tf_op jit(solution)/shard_map/ppermute | solution.py:636
  12.0 12.0 %collective-permute-start.1 = (bf16[1,16,16,128]{3,2,1,0:T(8,128)(2,1)S(1)}, bf16[1,16,16,128]{3,2,1,0:T(8,128)(2,1)S(1)}, u32[]{:S(2)}, u32[]{:S(2)}) collective-permute-start(bf16[1,16,16,128]{3,2,1,0:T(8,128)(2,1)S(1)} %get-tuple-element.28), channel_id=1, source_target_pairs={{1,2},{3,4},{5,6},{7,8},{9,10},{11,12},{13,14},{2,1},{4,3},{6,5},{... | collective-permute-start | bytes 196616 | tf_op jit(solution)/shard_map/ppermute | solution.py:638
  18.3 8.2 %all-to-all-start.1 = ((f32[16,2,128]{2,1,0:T(2,128)}), f32[16,2,128]{2,1,0:T(2,128)S(1)}, u32[]{:S(2)}, u32[]{:S(2)}) async-start(f32[16,2,128]{2,1,0:T(2,128)} %get-tuple-element.24), calls=%async_computation.1 | async-start | bytes 32768 | tf_op jit(solution)/shard_map/all_to_all | solution.py:639

commit v2 on v1

--- a/solution.py
+++ b/solution.py
@@ -341,18 +341,21 @@
     return pltpu.with_memory_space_constraint(array, pltpu.HBM)
 
 
+def tap_lane(j, k, e):
+    return (j + 1) * PATCH + 4 * k + e
+
+
 def prepare_kernel(out_weight, wide, scratch):
-    block = scratch.shape[0] // 3
     amount = scratch.shape[1] // LANES
-    span = 3 * (amount + 2)
     scratch[...] = jnp.zeros_like(scratch)
     for a in range(3):
         for e in range(3):
             for b in range(3):
                 piece = out_weight[a, b, e].astype(F32)
                 for i in range(amount):
-                    start = a * block + e * span + 3 * (i - b + 2)
-                    scratch[start : start + 3, i * LANES : (i + 1) * LANES] = piece
+                    for k in range(3):
+                        at = a * LANES + tap_lane(i - b + 2, k, e)
+                        scratch[at : at + 1, i * LANES : (i + 1) * LANES] = piece[k : k + 1]
     wide[...] = scratch[...].astype(BF16)
 
 
@@ -372,60 +375,73 @@
 
 
 def slope_kernel(
-    owner, arrived, hidden, gain, shift, wide, direct, edge_slopes, stats, sums, slopes_own, received
+    owner, arrived, hidden, gain, shift, wide, direct, edge_slopes, stats, sums, slopes_own, received, taps
 ):
     devices, message_rows, _ = arrived.shape
     own_rows, frame_count, width, channels = hidden.shape
     cells = frame_count * width
     per_frame = devices // frame_count
-    received[...] = arrived[...].reshape(received.shape)
-
-    def from_all(row):
-        return received[pl.ds(row, devices, stride=message_rows), :]
-
-    totals = jnp.sum(from_all(3), axis=0, keepdims=True)
+    got = arrived[...].reshape(received.shape)
+    kind = mod(iota((got.shape[0], 1), 0), message_rows)
+    totals = jnp.sum(jnp.where(kind == 3, got, 0.0), axis=0, keepdims=True)
     mean, inverse = norm_constants(totals, own_rows * devices * cells * (channels // GROUPS))
     for i in range(own_rows):
         state = hidden[i].reshape(cells, channels).astype(F32)
         slopes_own[i] = norm_slopes(state, mean, inverse, gain[...], shift[...])[1]
 
-    lines = jnp.concatenate([from_all(k) for k in range(3)], axis=1).astype(BF16)
-    place = iota((1, devices), 1)
-    source = jnp.zeros_like(place)
-    for index, d in enumerate(first_order(devices)):
-        source = jnp.where(place == index, d, source)
-    home = jnp.zeros((1, devices), jnp.int32)
-    for b in range(frame_count):
-        home = jnp.where(div(source, per_frame) == b, owner[b] * per_frame, home)
-    home = home + mod(source, per_frame)
-    cell = iota((cells, 1), 0)
-    column = mod(cell, width)
-    frame_strip = div(cell, width) * per_frame
-    lane = mod(iota((1, 3 * LANES), 1), PATCH)
-    kept = []
-    placed = None
-    for e in range(3):
-        wanted = column - e + 1
-        if per_frame > 1 or placed is None:
-            strip = frame_strip + div(wanted, PATCH) if per_frame > 1 else frame_strip
+    if per_frame == 1:
+        lane = iota((1, LANES), 1)
+        entry = iota((LANES, 1), 0)
+        turned = ones_where(entry - mod(entry, PATCH) + PATCH - 1 - mod(entry, PATCH) == lane)
+        received[...] = matmul(jnp.where(kind < 3, got, 0.0).astype(BF16), turned)
+        lane = mod(iota((PATCH, LANES), 1), PATCH)
+        column = iota((PATCH, LANES), 0)
+        marks = []
+        for k in range(3):
+            e = lane - 4 * k
+            wanted = column - e + 1
+            marks.append((e >= 0) & (e < 3) & (wanted >= 0) & (wanted < PATCH))
+        for d in range(devices):
+            row = first_order(devices)[d]
+            block = jnp.zeros((PATCH, LANES), F32)
+            for k in range(3):
+                line = jnp.broadcast_to(received[d * message_rows + k : d * message_rows + k + 1, :], (PATCH, LANES))
+                line = pltpu.roll(line, 4 * k + 2, 1, stride=1, stride_axis=0)
+                block = jnp.where(marks[k], line, block)
+            start = pl.multiple_of(owner[row] * PATCH, PATCH)
+            taps[pl.ds(start, PATCH), :] = block.astype(BF16)
+    else:
+        received[...] = got
+        lines = [received[pl.ds(k, devices, stride=message_rows), :] for k in range(3)]
+        lines = jnp.concatenate(lines, axis=1).astype(BF16)
+        place = iota((1, devices), 1)
+        source = jnp.zeros_like(place)
+        for index, d in enumerate(first_order(devices)):
+            source = jnp.where(place == index, d, source)
+        home = jnp.zeros((1, devices), jnp.int32)
+        for b in range(frame_count):
+            home = jnp.where(div(source, per_frame) == b, owner[b] * per_frame, home)
+        home = home + mod(source, per_frame)
+        cell = iota((cells, 1), 0)
+        column = mod(cell, width)
+        lane = mod(iota((1, 3 * LANES), 1), PATCH)
+        entry = iota((3 * LANES, 1), 0)
+        window_row = div(mod(entry, LANES), PATCH)
+        found = jnp.zeros((cells, LANES), F32)
+        for e in range(3):
+            wanted = column - e + 1
+            strip = div(cell, width) * per_frame + div(wanted, PATCH)
             placed = matmul(ones_where(home == strip), lines)
-        inside = jnp.where((wanted >= 0) & (wanted < width), mod(wanted, PATCH), -1)
-        kept.append(jnp.where(lane == inside, placed, 0.0).astype(BF16))
-    block = wide.shape[0] // 3
-    span = 3 * (own_rows + 4)
-    entry = iota((3 * LANES, 1), 0)
-    entry = div(mod(entry, LANES), PATCH) * 3 + div(entry, LANES)
-    entry = jnp.where(entry < span, entry, -3 * span)
-    tap = iota((1, block), 1)
-    folds = jnp.concatenate([ones_where(tap == entry + e * span) for e in range(3)], axis=0)
-    taps = matmul(jnp.concatenate(kept, axis=1), folds).astype(BF16)
-    later = []
-    for a in range(3):
-        skip = (2 - a) * width
-        later.append(
-            jnp.concatenate([taps[skip:], jnp.zeros((skip, block), BF16)], axis=0) if skip else taps
-        )
-    result = matmul(jnp.concatenate(later, axis=1), wide[...])
+            inside = jnp.where((wanted >= 0) & (wanted < width), mod(wanted, PATCH), -1)
+            kept = jnp.where(lane == inside, placed, 0.0).astype(BF16)
+            target = jnp.where(
+                window_row < own_rows + 4, tap_lane(window_row, div(entry, LANES), e), -1
+            )
+            found = found + matmul(kept, ones_where(target == iota((1, LANES), 1)))
+        taps[:cells, :] = found.astype(BF16)
+    taps[cells:, :] = jnp.zeros((2 * width, LANES), BF16)
+    steps = [taps[(2 - a) * width : (2 - a) * width + cells, :] for a in range(3)]
+    result = matmul(jnp.concatenate(steps, axis=1), wide[...])
 
     first = jnp.zeros((1, channels), F32)
     second = jnp.zeros((1, channels), F32)
@@ -548,7 +564,6 @@
     head_bias_row = head_bias.reshape(1, width)
     head_out_row = head_out.reshape(1, width)
     state_rows = own_rows + 2
-    tap_rows = -(-9 * (own_rows + 4) // LANES) * LANES
     edge = jax.ShapeDtypeStruct((1,) + hidden_state.shape[1:], BF16)
     message = (message_shape(devices), edge, edge)
     gain_row = group_gain.reshape(1, channels)
@@ -614,9 +629,9 @@
     early = [near(x) for x in early]
     wide = pl.pallas_call(
         prepare_kernel,
-        out_shape=pltpu.VMEM((3 * tap_rows, state_rows * channels), BF16),
+        out_shape=pltpu.VMEM((3 * LANES, state_rows * channels), BF16),
         in_specs=[VMEM],
-        scratch_shapes=[pltpu.VMEM((3 * tap_rows, state_rows * channels), F32)],
+        scratch_shapes=[pltpu.VMEM((3 * LANES, state_rows * channels), F32)],
         compiler_params=params(cells),
         name="prepare",
     )(early[3])
@@ -628,6 +643,7 @@
         scratch_shapes=[
             pltpu.VMEM((own_rows, cells, channels), F32),
             pltpu.VMEM((4 * devices, LANES), F32),
+            pltpu.VMEM((cells + 2 * frame_width, LANES), BF16),
         ],
         compiler_params=params(cells),
         name="slope",

time: 28.7 us -> 28.6 us (level)
  no operation moved by 1% of the time
where the time goes in v2:
time: 28.6 us; the launch traced here: 28.3 us
  starting transfers between devices  14.1 us (49%)
  Pallas kernels  9.8 us (34%)
  waiting for transfers between devices  4.32 us (15%)
    all_to_all x1, starting transfers between devices, per_device(): lax.all_to_all(send, 'row', 0, 0, axis_index_groups=[first_order(devices)...  7.6 us
    all_to_all x1, starting transfers between devices, per_device(): lax.all_to_all(sums, 'row', 0, 0, axis_index_groups=[led_by(devices - 1,...  5.77 us
    pallas_call x1, Pallas kernels, per_device(): pl.pallas_call(reward_kernel, out_shape=message + tuple((pltpu.VMEM(x.sha...  4.34 us
    all_to_all x1, waiting for transfers between devices, per_device(): lax.all_to_all(send, 'row', 0, 0, axis_index_groups=[first_order(devices)...  3.43 us
    pallas_call x1, Pallas kernels, per_device(): pl.pallas_call(functools.partial(inner_kernel, devices=devices), out_shap...  2.02 us
    pallas_call x1, Pallas kernels, per_device(): pl.pallas_call(slope_kernel, out_shape=slope_outs, in_specs=[SMEM] + [VME...  1.78 us
    pallas_call x1, Pallas kernels, per_device(): pl.pallas_call(late_kernel, out_shape=(pltpu.VMEM((2, cells, channels), F...  1.47 us
    all_to_all x1, waiting for transfers between devices, per_device(): lax.all_to_all(sums, 'row', 0, 0, axis_index_groups=[led_by(devices - 1,...  0.89 us
  transfers between devices with their start and end apart: 4, of which 2 were waited for; matrix products, arithmetic and copies ran while one was open for 0% of the time, Pallas kernels for 12%

profile of v2, /device:TPU:0, one launch (start us, length us, event | category | flops | bytes accessed | tf_op | source)
XLA Modules:
  0.0 28.3 jit_solution(16499947091651163043)
XLA Ops:
  0.0 0.0 copy-start
  0.0 4.3 %reward.1 = (f32[16,4,128]{2,1,0:T(4,128)}, bf16[1,16,16,128]{3,2,1,0:T(8,128)(2,1)S(1)}, bf16[1,16,16,128]{3,2,1,0:T(8,128)(2,1)S(1)}, bf16[3,16,16,128]{3,2,1,...) custom-call(s32[1]{0:T(128)} %bitcast.place, ...), custom_call_target="tpu_custom_call" | custom-call | tf_op jit(solution)/shard_map/reward/pallas_call | solution.py:585
  4.3 7.6 %all-to-all-start = ((f32[16,4,128]{2,1,0:T(4,128)}), f32[16,4,128]{2,1,0:T(4,128)S(1)}, u32[]{:S(2)}, u32[]{:S(2)}) async-start(f32[16,4,128]{2,1,0:T(4,128)} %get-tuple-element.19), calls=%async_computation | async-start | bytes 65536 | tf_op jit(solution)/shard_map/all_to_all | solution.py:638
  12.0 0.1 collective-permute-start
  12.0 0.7 %collective-permute-start.1 = (bf16[1,16,16,128]{3,2,1,0:T(8,128)(2,1)S(1)}, bf16[1,16,16,128]{3,2,1,0:T(8,128)(2,1)S(1)}, u32[]{:S(2)}, u32[]{:S(2)}) collective-permute-start(bf16[1,16,16,128]{3,2,1,0:T(8,128)(2,1)S(1)} %get-tuple-element.28), channel_id=1, source_target_pairs={{1,2},{3,4},{5,6},{7,8},{9,10},{11,12},{13,14},{2,1},{4,3},{6,5},{... | collective-permute-start | bytes 196616 | tf_op jit(solution)/shard_map/ppermute | solution.py:654
  12.7 0.2 prepare.1.wide
  12.9 3.4 %all-to-all-done.arrived = f32[16,4,128]{2,1,0:T(4,128)S(1)} async-done(((f32[16,4,128]{2,1,0:T(4,128)}), f32[16,4,128]{2,1,0:T(4,128)S(1)}, u32[]{:S(2)}, u32[]{:S(2)}) %all-to-all-start) | async-done | bytes 32800 | tf_op jit(solution)/shard_map/all_to_all | solution.py:638
  16.3 0.0 copy-done
  16.3 1.8 %slope.1 = (f32[3,256,128]{2,1,0:T(8,128)S(1)}, f32[2,256,128]{2,1,0:T(8,128)S(1)}, f32[8,128]{1,0:T(8,128)S(1)}, f32[16,2,128]{2,1,0:T(2,128)}) custom-call(s32[16]{0:T(128)S(1)} %copy-done, f32[16,4,128]{2,1,0:T(4,128)S(1)} %all-to-all-done.arrived, bf16[3,16,16,128]{3,2,1,0:T(8,128)(2,1)S(1)} %get-tuple-element.20.hidden, ...), custom_call_target="tpu_custom_call" | custom-call | tf_op jit(solution)/shard_map/slope/pallas_call | solution.py:639
  18.1 5.8 %all-to-all-start.1 = ((f32[16,2,128]{2,1,0:T(2,128)}), f32[16,2,128]{2,1,0:T(2,128)S(1)}, u32[]{:S(2)}, u32[]{:S(2)}) async-start(f32[16,2,128]{2,1,0:T(2,128)} %get-tuple-element.24), calls=%async_computation.1 | async-start | bytes 32768 | tf_op jit(solution)/shard_map/all_to_all | solution.py:655
  23.9 0.0 collective-permute-done.across
  23.9 0.0 collective-permute-done.1.along
  23.9 1.5 %late.1 = (f32[2,256,128]{2,1,0:T(8,128)S(1)}, bf16[2,16,16,128]{3,2,1,0:T(8,128)(2,1)S(1)}, bf16[1152,384]{1,0:T(8,128)(2,1)S(1)}) custom-call(s32[1]{0:T(128)} %bitcast.place, bf16[1,16,16,128]{3,2,1,0:T(8,128)(2,1)S(1)} %collective-permute-done.across, bf16[1,16,16,128]{3,2,1,0:T(8,128)(2,1)S(1)} %collective-permute-done.1.along, ...), custom_call_target="tpu_custom_call", output_to_operand_aliasing={{0}: (3, {})} | custom-call | tf_op jit(solution)/shard_map/late/pallas_call | solution.py:656
  25.4 0.9 %all-to-all-done.1.arrived = f32[16,2,128]{2,1,0:T(2,128)S(1)} async-done(((f32[16,2,128]{2,1,0:T(2,128)}), f32[16,2,128]{2,1,0:T(2,128)S(1)}, u32[]{:S(2)}, u32[]{:S(2)}) %all-to-all-start.1) | async-done | bytes 16416 | tf_op jit(solution)/shard_map/all_to_all | solution.py:655
  26.3 2.0 %inner.1 = bf16[3,16,16,128]{3,2,1,0:T(8,128)(2,1)} custom-call(s32[1]{0:T(128)} %bitcast.place, f32[16,2,128]{2,1,0:T(2,128)S(1)} %all-to-all-done.1.arrived, f32[8,128]{1,0:T(8,128)S(1)} %get-tuple-element.25.stats, f32[3,256,128]{2,1,0:T(8,128)S(1)} %get-tuple-element.26.direct, bf16[3,16,16,128]{3,2,1,0:T(8,128)(2,1)S(1)} %get-tuple-element.20.hidden, ...), custom_call_target="tpu_custom_call" | custom-call | tf_op jit(solution)/shard_map/inner/pallas_call | solution.py:669
Async XLA Ops:
  0.0 16.3 %copy-start = (s32[16]{0:T(128)S(1)}, s32[16]{0:T(128)}, u32[]{:S(2)}) copy-start(s32[16]{0:T(128)} %owner.1) | copy-start | bytes 196
  4.3 12.0 %all-to-all-start = ((f32[16,4,128]{2,1,0:T(4,128)}), f32[16,4,128]{2,1,0:T(4,128)S(1)}, u32[]{:S(2)}, u32[]{:S(2)}) async-start(f32[16,4,128]{2,1,0:T(4,128)} %get-tuple-element.19), calls=%async_computation | async-start | bytes 65536 | tf_op jit(solution)/shard_map/all_to_all | solution.py:638
  12.0 11.9 %collective-permute-start = (bf16[1,16,16,128]{3,2,1,0:T(8,128)(2,1)S(1)}, bf16[1,16,16,128]{3,2,1,0:T(8,128)(2,1)S(1)}, u32[]{:S(2)}, u32[]{:S(2)}) collective-permute-start(bf16[1,16,16,128]{3,2,1,0:T(8,128)(2,1)S(1)} %get-tuple-element.27), channel_id=1, source_target_pairs={{0,1},{2,3},{4,5},{6,7},{8,9},{10,11},{12,13},{14,15},{1,0},{3,2},... | collective-permute-start | bytes 196616 | tf_op jit(solution)/shard_map/ppermute | solution.py:652
  12.0 11.8 %collective-permute-start.1 = (bf16[1,16,16,128]{3,2,1,0:T(8,128)(2,1)S(1)}, bf16[1,16,16,128]{3,2,1,0:T(8,128)(2,1)S(1)}, u32[]{:S(2)}, u32[]{:S(2)}) collective-permute-start(bf16[1,16,16,128]{3,2,1,0:T(8,128)(2,1)S(1)} %get-tuple-element.28), channel_id=1, source_target_pairs={{1,2},{3,4},{5,6},{7,8},{9,10},{11,12},{13,14},{2,1},{4,3},{6,5},{... | collective-permute-start | bytes 196616 | tf_op jit(solution)/shard_map/ppermute | solution.py:654
  18.1 8.2 %all-to-all-start.1 = ((f32[16,2,128]{2,1,0:T(2,128)}), f32[16,2,128]{2,1,0:T(2,128)S(1)}, u32[]{:S(2)}, u32[]{:S(2)}) async-start(f32[16,2,128]{2,1,0:T(2,128)} %get-tuple-element.24), calls=%async_computation.1 | async-start | bytes 32768 | tf_op jit(solution)/shard_map/all_to_all | solution.py:655

commit v3 on v2

--- a/solution.py
+++ b/solution.py
@@ -100,9 +100,10 @@
 
 
 def forward_part(tokens, count, bias, gain, load_patch):
-    embedded = bias[...]
+    embedded = jnp.zeros((tokens.shape[0], bias.shape[1]), F32)
     for low, high, weight in load_patch():
         embedded = embedded + matmul(tokens[:, low:high], weight)
+    embedded = embedded + bias[...]
     centred = embedded - jnp.mean(embedded, axis=1, keepdims=True)
     inv_spread = lax.rsqrt(jnp.mean(centred * centred, axis=1, keepdims=True) + eps_norm)
     normed = centred * inv_spread
@@ -201,14 +202,15 @@
     write_windows(patch_grad, sums, own_rows, height, send)
 
 
-def write_edges(place, hidden, across, along):
+def write_edges(position, hidden, across, along):
     last = hidden.shape[0] - 1
-    even = place[0] % 2 == 0
+    even = position % 2 == 0
     across[0] = hidden[jnp.where(even, last, 0)]
     along[0] = hidden[jnp.where(even, 0, last)]
 
 
-def reward_kernel(place, *refs):
+def reward_kernel(*refs):
+    position = lax.axis_index("row")
     count, kept = 7, 4
     far, refs = refs[: count + kept + 2], refs[count + kept + 2 :]
     send, across, along = refs[:3]
@@ -216,7 +218,7 @@
     sems = refs[-1]
     frames, bias, gain, owner, picks, head_bias, head_out, hidden, _, _, _, patch, head = near
     count += kept
-    depth, depths = 256, (128, 256)
+    depth, depths = 256, (256, 256)
     small = [pltpu.make_async_copy(far[i], near[i], sems.at[i]) for i in range(count)]
     pieces = []
     used = count
@@ -228,7 +230,7 @@
             parts.append(pltpu.make_async_copy(source.at[part], target.at[part], sems.at[used]))
             used += 1
         pieces.append(parts)
-    for copy in [small[0], small[7], small[1]] + pieces[0] + small[2:7] + pieces[1] + small[8:]:
+    for copy in [small[0], small[7]] + pieces[0] + small[1:7] + pieces[1] + small[8:]:
         copy.start()
 
     def load_patch():
@@ -236,6 +238,8 @@
             for copy in pieces[0][low // depths[0] : (low + depth) // depths[0]]:
                 copy.wait()
             yield low, low + depth, patch[low : low + depth, :]
+        small[1].wait()
+        small[2].wait()
 
     height = frames.shape[2]
     patches = height // PATCH
@@ -243,9 +247,7 @@
     small[7].wait()
     tokens = to_tokens(frames[...])
     sums = group_sums(hidden[...])
-    write_edges(place, hidden, across, along)
-    small[1].wait()
-    small[2].wait()
+    write_edges(position, hidden, across, along)
     normed, inv_spread, pooled = forward_part(tokens, patches, bias, gain, load_patch)
     for copy in small[3:7]:
         copy.wait()
@@ -269,7 +271,7 @@
         patch,
         head,
         through_head,
-        place[0],
+        position,
         hidden.shape[0],
         height,
         sums,
@@ -291,7 +293,6 @@
 def backward_kernel(
     owner,
     picks,
-    place,
     hidden,
     gain,
     head_bias,
@@ -308,7 +309,8 @@
     height,
     per_frame,
 ):
-    write_edges(place, hidden, across, along)
+    position = lax.axis_index("row")
+    write_edges(position, hidden, across, along)
     backward_part(
         owner,
         picks,
@@ -321,7 +323,7 @@
         patch,
         head,
         lambda rows: matmul(rows, head[...]),
-        place[0] // per_frame,
+        position // per_frame,
         hidden.shape[0],
         height,
         group_sums(hidden[...]),
@@ -375,8 +377,24 @@
 
 
 def slope_kernel(
-    owner, arrived, hidden, gain, shift, wide, direct, edge_slopes, stats, sums, slopes_own, received, taps
+    arrived,
+    hidden,
+    gain,
+    shift,
+    wide,
+    far_owner,
+    direct,
+    edge_slopes,
+    stats,
+    sums,
+    slopes_own,
+    received,
+    taps,
+    owner,
+    sem,
 ):
+    copy = pltpu.make_async_copy(far_owner, owner, sem.at[0])
+    copy.start()
     devices, message_rows, _ = arrived.shape
     own_rows, frame_count, width, channels = hidden.shape
     cells = frame_count * width
@@ -387,7 +405,7 @@
     mean, inverse = norm_constants(totals, own_rows * devices * cells * (channels // GROUPS))
     for i in range(own_rows):
         state = hidden[i].reshape(cells, channels).astype(F32)
-        slopes_own[i] = norm_slopes(state, mean, inverse, gain[...], shift[...])[1]
+        slopes_own[i] = norm_slopes(state, mean, inverse, gain[...], shift[...])[1] * inverse
 
     if per_frame == 1:
         lane = iota((1, LANES), 1)
@@ -401,6 +419,7 @@
             e = lane - 4 * k
             wanted = column - e + 1
             marks.append((e >= 0) & (e < 3) & (wanted >= 0) & (wanted < PATCH))
+        copy.wait()
         for d in range(devices):
             row = first_order(devices)[d]
             block = jnp.zeros((PATCH, LANES), F32)
@@ -411,6 +430,7 @@
             start = pl.multiple_of(owner[row] * PATCH, PATCH)
             taps[pl.ds(start, PATCH), :] = block.astype(BF16)
     else:
+        copy.wait()
         received[...] = got
         lines = [received[pl.ds(k, devices, stride=message_rows), :] for k in range(3)]
         lines = jnp.concatenate(lines, axis=1).astype(BF16)
@@ -447,10 +467,11 @@
     second = jnp.zeros((1, channels), F32)
     for i in range(own_rows):
         state = hidden[i].reshape(cells, channels).astype(F32)
-        up = result[:, (i + 1) * channels : (i + 2) * channels] * slopes_own[i]
-        direct[i] = up * inverse
-        first = first + jnp.sum(up, axis=0, keepdims=True)
-        second = second + jnp.sum(up * ((state - mean) * inverse), axis=0, keepdims=True)
+        part = result[:, (i + 1) * channels : (i + 2) * channels] * slopes_own[i]
+        direct[i] = part
+        first = first + jnp.sum(part, axis=0, keepdims=True)
+        second = second + jnp.sum(part * (state - mean), axis=0, keepdims=True)
+    first = first / inverse
     edge_slopes[0] = result[:, :channels]
     edge_slopes[1] = result[:, (own_rows + 1) * channels :]
     stats[0:1, :] = mean
@@ -460,12 +481,12 @@
 
 
 def late_kernel(
-    place, across, along, slopes, stats, gain, shift, far_weight, direct, states, turned, inner_weight, sem
+    across, along, slopes, stats, gain, shift, far_weight, direct, states, turned, inner_weight, sem
 ):
     copy = pltpu.make_async_copy(far_weight, inner_weight, sem.at[0])
     copy.start()
     cells, channels = slopes.shape[1:]
-    odd = place[0] % 2 == 1
+    odd = lax.axis_index("row") % 2 == 1
     mean = stats[0:1, :]
     inverse = stats[1:2, :]
     for i in range(2):
@@ -483,7 +504,7 @@
 
 
 def inner_kernel(
-    place, arrived, stats, direct, hidden, edge_direct, edge_states, turned, far_out, padded, out, sems, *, devices
+    arrived, stats, direct, hidden, edge_direct, edge_states, turned, far_out, padded, out, sems, *, devices
 ):
     own_rows, frame_count, width, channels = out.shape
     cells = frame_count * width
@@ -497,7 +518,7 @@
     inverse = stats[1:2, :]
     constant = first / cell_total * inverse
     factor = second / cell_total * inverse * inverse
-    position = place[0]
+    position = lax.axis_index("row")
     in_frame = mod(iota((cells, 1), 0), width)
     for i in range(own_rows + 2):
         if 0 < i < own_rows + 1:
@@ -552,7 +573,6 @@
     inner_weight,
 ):
     devices = lax.axis_size("row")
-    position = lax.axis_index("row").astype(jnp.int32).reshape(1)
     per_frame = devices // FRAMES
     height = frames.shape[1]
     own_rows, _, frame_width, channels = hidden_state.shape
@@ -585,12 +605,12 @@
         send, across, along, *early = pl.pallas_call(
             reward_kernel,
             out_shape=message + tuple(pltpu.VMEM(x.shape, x.dtype) for x in early),
-            in_specs=[SMEM] + [FAR] * (len(arrays) + len(early) + len(weights)),
+            in_specs=[FAR] * (len(arrays) + len(early) + len(weights)),
             out_specs=[VMEM] * (3 + len(early)),
             scratch_shapes=[scratch(x) for x in arrays + weights] + [pltpu.SemaphoreType.DMA((32,))],
             compiler_params=params(0),
             name="reward",
-        )(position, *[far(x) for x in arrays + early + weights])
+        )(*[far(x) for x in arrays + early + weights])
     else:
         count = height // PATCH
         normed, inv_spread, partial = pl.pallas_call(
@@ -608,14 +628,13 @@
         send, across, along = pl.pallas_call(
             functools.partial(backward_kernel, height=height, per_frame=per_frame),
             out_shape=message,
-            in_specs=[SMEM] * 3 + [VMEM] * 9,
+            in_specs=[SMEM] * 2 + [VMEM] * 9,
             out_specs=[VMEM] * 3,
             compiler_params=params(cells),
             name="reward_backward",
         )(
             frame_owner,
             picks,
-            position,
             hidden_state,
             gain,
             head_bias_row,
@@ -639,15 +658,17 @@
     direct, edge_slopes, stats, sums = pl.pallas_call(
         slope_kernel,
         out_shape=slope_outs,
-        in_specs=[SMEM] + [VMEM] * 5,
+        in_specs=[VMEM] * 5 + [FAR],
         scratch_shapes=[
             pltpu.VMEM((own_rows, cells, channels), F32),
             pltpu.VMEM((4 * devices, LANES), F32),
             pltpu.VMEM((cells + 2 * frame_width, LANES), BF16),
+            pltpu.SMEM(frame_owner.shape, jnp.int32),
+            pltpu.SemaphoreType.DMA((1,)),
         ],
         compiler_params=params(cells),
         name="slope",
-    )(frame_owner, near(arrived), *early[:3], near(wide))
+    )(near(arrived), *early[:3], near(wide), far(frame_owner))
     swaps = [(2 * i, 2 * i + 1) for i in range(devices // 2)]
     across = lax.ppermute(across, "row", swaps + [(b, a) for a, b in swaps])
     swaps = [(2 * i - 1, 2 * i) for i in range(1, devices // 2)]
@@ -660,16 +681,16 @@
             pltpu.VMEM((2,) + hidden_state.shape[1:], BF16),
             pltpu.VMEM((9 * channels, 3 * channels), BF16),
         ),
-        in_specs=[SMEM] + [VMEM] * 6 + [FAR],
+        in_specs=[VMEM] * 6 + [FAR],
         scratch_shapes=[pltpu.VMEM(inner_weight.shape, BF16), pltpu.SemaphoreType.DMA((1,))],
-        input_output_aliases={3: 0},
+        input_output_aliases={2: 0},
         compiler_params=params(cells),
         name="late",
-    )(position, near(across), near(along), near(edge_slopes), near(stats), *early[1:3], far(inner_weight))
+    )(near(across), near(along), near(edge_slopes), near(stats), *early[1:3], far(inner_weight))
     return pl.pallas_call(
         functools.partial(inner_kernel, devices=devices),
         out_shape=jax.ShapeDtypeStruct(hidden_state.shape, BF16),
-        in_specs=[SMEM] + [VMEM] * 7,
+        in_specs=[VMEM] * 7,
         out_specs=FAR,
         scratch_shapes=[
             pltpu.VMEM((own_rows + 2, cells + 2 * frame_width, 3 * channels), BF16),
@@ -679,7 +700,6 @@
         compiler_params=params(cells),
         name="inner",
     )(
-        position,
         near(summed),
         near(stats),
         near(direct),

time: 28.6 us -> 28.5 us (level)
  no operation moved by 1% of the time
where the time goes in v3:
time: 28.5 us; the launch traced here: 28.2 us
  starting transfers between devices  14.1 us (49%)
  Pallas kernels  9.72 us (34%)
  waiting for transfers between devices  4.33 us (15%)
    all_to_all x1, starting transfers between devices, per_device(): lax.all_to_all(send, 'row', 0, 0, axis_index_groups=[first_order(devices)...  7.6 us
    all_to_all x1, starting transfers between devices, per_device(): lax.all_to_all(sums, 'row', 0, 0, axis_index_groups=[led_by(devices - 1,...  5.78 us
    pallas_call x1, Pallas kernels, per_device(): pl.pallas_call(reward_kernel, out_shape=message + tuple((pltpu.VMEM(x.sha...  4.36 us
    all_to_all x1, waiting for transfers between devices, per_device(): lax.all_to_all(send, 'row', 0, 0, axis_index_groups=[first_order(devices)...  3.43 us
    pallas_call x1, Pallas kernels, per_device(): pl.pallas_call(functools.partial(inner_kernel, devices=devices), out_shap...  2.02 us
    pallas_call x1, Pallas kernels, per_device(): pl.pallas_call(slope_kernel, out_shape=slope_outs, in_specs=[VMEM] * 5 +...  1.69 us
    pallas_call x1, Pallas kernels, per_device(): pl.pallas_call(late_kernel, out_shape=(pltpu.VMEM((2, cells, channels), F...  1.47 us
    all_to_all x1, waiting for transfers between devices, per_device(): lax.all_to_all(sums, 'row', 0, 0, axis_index_groups=[led_by(devices - 1,...  0.89 us
  transfers between devices with their start and end apart: 4, of which 2 were waited for; matrix products, arithmetic and copies ran while one was open for 0% of the time, Pallas kernels for 12%

profile of v3, /device:TPU:0, one launch (start us, length us, event | category | flops | bytes accessed | tf_op | source)
XLA Modules:
  0.0 28.2 jit_solution(5754362707874104932)
XLA Ops:
  0.0 4.4 %reward.1 = (f32[16,4,128]{2,1,0:T(4,128)}, bf16[1,16,16,128]{3,2,1,0:T(8,128)(2,1)S(1)}, bf16[1,16,16,128]{3,2,1,0:T(8,128)(2,1)S(1)}, bf16[3,16,16,128]{3,2,1,...) custom-call(bf16[3,16,48]{2,1,0:T(8,128)(2,1)} %bitcast.7, ...), custom_call_target="tpu_custom_call" | custom-call | tf_op jit(solution)/shard_map/reward/pallas_call | solution.py:605
  4.4 7.6 %all-to-all-start = ((f32[16,4,128]{2,1,0:T(4,128)}), f32[16,4,128]{2,1,0:T(4,128)S(1)}, u32[]{:S(2)}, u32[]{:S(2)}) async-start(f32[16,4,128]{2,1,0:T(4,128)} %get-tuple-element.19), calls=%async_computation | async-start | bytes 65536 | tf_op jit(solution)/shard_map/all_to_all | solution.py:657
  12.0 0.1 collective-permute-start
  12.1 0.7 %collective-permute-start.1 = (bf16[1,16,16,128]{3,2,1,0:T(8,128)(2,1)S(1)}, bf16[1,16,16,128]{3,2,1,0:T(8,128)(2,1)S(1)}, u32[]{:S(2)}, u32[]{:S(2)}) collective-permute-start(bf16[1,16,16,128]{3,2,1,0:T(8,128)(2,1)S(1)} %get-tuple-element.28), channel_id=1, source_target_pairs={{1,2},{3,4},{5,6},{7,8},{9,10},{11,12},{13,14},{2,1},{4,3},{6,5},{... | collective-permute-start | bytes 196616 | tf_op jit(solution)/shard_map/ppermute | solution.py:675
  12.7 0.2 prepare.1.wide
  12.9 3.4 %all-to-all-done.arrived = f32[16,4,128]{2,1,0:T(4,128)S(1)} async-done(((f32[16,4,128]{2,1,0:T(4,128)}), f32[16,4,128]{2,1,0:T(4,128)S(1)}, u32[]{:S(2)}, u32[]{:S(2)}) %all-to-all-start) | async-done | bytes 32800 | tf_op jit(solution)/shard_map/all_to_all | solution.py:657
  16.3 1.7 %slope.1 = (f32[3,256,128]{2,1,0:T(8,128)S(1)}, f32[2,256,128]{2,1,0:T(8,128)S(1)}, f32[8,128]{1,0:T(8,128)S(1)}, f32[16,2,128]{2,1,0:T(2,128)}) custom-call(f32[16,4,128]{2,1,0:T(4,128)S(1)} %all-to-all-done.arrived, bf16[3,16,16,128]{3,2,1,0:T(8,128)(2,1)S(1)} %get-tuple-element.20.hidden, f32[1,128]{1,0:T(1,128)S(1)} %get-tuple-element.21.gain, ...), custom_call_target="tpu_custom_call" | custom-call | tf_op jit(solution)/shard_map/slope/pallas_call | solution.py:658
  18.0 5.8 %all-to-all-start.1 = ((f32[16,2,128]{2,1,0:T(2,128)}), f32[16,2,128]{2,1,0:T(2,128)S(1)}, u32[]{:S(2)}, u32[]{:S(2)}) async-start(f32[16,2,128]{2,1,0:T(2,128)} %get-tuple-element.24), calls=%async_computation.1 | async-start | bytes 32768 | tf_op jit(solution)/shard_map/all_to_all | solution.py:676
  23.8 0.0 collective-permute-done.across
  23.8 0.0 collective-permute-done.1.along
  23.8 1.5 %late.1 = (f32[2,256,128]{2,1,0:T(8,128)S(1)}, bf16[2,16,16,128]{3,2,1,0:T(8,128)(2,1)S(1)}, bf16[1152,384]{1,0:T(8,128)(2,1)S(1)}) custom-call(bf16[1,16,16,128]{3,2,1,0:T(8,128)(2,1)S(1)} %collective-permute-done.across, bf16[1,16,16,128]{3,2,1,0:T(8,128)(2,1)S(1)} %collective-permute-done.1.along, ...), custom_call_target="tpu_custom_call", output_to_operand_aliasing={{0}: (2, {})} | custom-call | tf_op jit(solution)/shard_map/late/pallas_call | solution.py:677
  25.3 0.9 %all-to-all-done.1.arrived = f32[16,2,128]{2,1,0:T(2,128)S(1)} async-done(((f32[16,2,128]{2,1,0:T(2,128)}), f32[16,2,128]{2,1,0:T(2,128)S(1)}, u32[]{:S(2)}, u32[]{:S(2)}) %all-to-all-start.1) | async-done | bytes 16416 | tf_op jit(solution)/shard_map/all_to_all | solution.py:676
  26.2 2.0 %inner.1 = bf16[3,16,16,128]{3,2,1,0:T(8,128)(2,1)} custom-call(f32[16,2,128]{2,1,0:T(2,128)S(1)} %all-to-all-done.1.arrived, f32[8,128]{1,0:T(8,128)S(1)} %get-tuple-element.25.stats, f32[3,256,128]{2,1,0:T(8,128)S(1)} %get-tuple-element.26.direct, bf16[3,16,16,128]{3,2,1,0:T(8,128)(2,1)S(1)} %get-tuple-element.20.hidden, ...), custom_call_target="tpu_custom_call" | custom-call | tf_op jit(solution)/shard_map/inner/pallas_call | solution.py:690
Async XLA Ops:
  4.4 12.0 %all-to-all-start = ((f32[16,4,128]{2,1,0:T(4,128)}), f32[16,4,128]{2,1,0:T(4,128)S(1)}, u32[]{:S(2)}, u32[]{:S(2)}) async-start(f32[16,4,128]{2,1,0:T(4,128)} %get-tuple-element.19), calls=%async_computation | async-start | bytes 65536 | tf_op jit(solution)/shard_map/all_to_all | solution.py:657
  12.0 11.8 %collective-permute-start = (bf16[1,16,16,128]{3,2,1,0:T(8,128)(2,1)S(1)}, bf16[1,16,16,128]{3,2,1,0:T(8,128)(2,1)S(1)}, u32[]{:S(2)}, u32[]{:S(2)}) collective-permute-start(bf16[1,16,16,128]{3,2,1,0:T(8,128)(2,1)S(1)} %get-tuple-element.27), channel_id=1, source_target_pairs={{0,1},{2,3},{4,5},{6,7},{8,9},{10,11},{12,13},{14,15},{1,0},{3,2},... | collective-permute-start | bytes 196616 | tf_op jit(solution)/shard_map/ppermute | solution.py:673
  12.1 11.8 %collective-permute-start.1 = (bf16[1,16,16,128]{3,2,1,0:T(8,128)(2,1)S(1)}, bf16[1,16,16,128]{3,2,1,0:T(8,128)(2,1)S(1)}, u32[]{:S(2)}, u32[]{:S(2)}) collective-permute-start(bf16[1,16,16,128]{3,2,1,0:T(8,128)(2,1)S(1)} %get-tuple-element.28), channel_id=1, source_target_pairs={{1,2},{3,4},{5,6},{7,8},{9,10},{11,12},{13,14},{2,1},{4,3},{6,5},{... | collective-permute-start | bytes 196616 | tf_op jit(solution)/shard_map/ppermute | solution.py:675
  18.0 8.2 %all-to-all-start.1 = ((f32[16,2,128]{2,1,0:T(2,128)}), f32[16,2,128]{2,1,0:T(2,128)S(1)}, u32[]{:S(2)}, u32[]{:S(2)}) async-start(f32[16,2,128]{2,1,0:T(2,128)} %get-tuple-element.24), calls=%async_computation.1 | async-start | bytes 32768 | tf_op jit(solution)/shard_map/all_to_all | solution.py:676

commit v4 on v3

--- a/solution.py
+++ b/solution.py
@@ -118,7 +118,7 @@
 
 
 def first_order(devices):
-    return led_by(devices * 9 // 16, devices)
+    return led_by(devices * 13 // 16, devices)
 
 
 def message_shape(devices):

time: 28.5 us -> 28.4 us (level)
  waiting for transfers between devices: 4.33 us -> 3.34 us
  starting transfers between devices: 14.1 us -> 15 us
    all_to_all x1, waiting for transfers between devices: 3.43 us -> 2.47 us  [per_device(): lax.all_to_all(send, 'row', 0, 0, axis_index_groups=[first_order(devices)...]
    all_to_all x1, starting transfers between devices: 5.78 us -> 6.35 us  [per_device(): lax.all_to_all(sums, 'row', 0, 0, axis_index_groups=[led_by(devices - 1,...]
    all_to_all x1, starting transfers between devices: 7.6 us -> 7.91 us  [per_device(): lax.all_to_all(send, 'row', 0, 0, axis_index_groups=[first_order(devices)...]
where the time goes in v4:
time: 28.4 us; the launch traced here: 28.1 us
  starting transfers between devices  15 us (53%)
  Pallas kernels  9.73 us (34%)
  waiting for transfers between devices  3.34 us (12%)
    all_to_all x1, starting transfers between devices, per_device(): lax.all_to_all(send, 'row', 0, 0, axis_index_groups=[first_order(devices)...  7.91 us
    all_to_all x1, starting transfers between devices, per_device(): lax.all_to_all(sums, 'row', 0, 0, axis_index_groups=[led_by(devices - 1,...  6.35 us
    pallas_call x1, Pallas kernels, per_device(): pl.pallas_call(reward_kernel, out_shape=message + tuple((pltpu.VMEM(x.sha...  4.36 us
    all_to_all x1, waiting for transfers between devices, per_device(): lax.all_to_all(send, 'row', 0, 0, axis_index_groups=[first_order(devices)...  2.47 us
    pallas_call x1, Pallas kernels, per_device(): pl.pallas_call(functools.partial(inner_kernel, devices=devices), out_shap...  2.02 us
    pallas_call x1, Pallas kernels, per_device(): pl.pallas_call(slope_kernel, out_shape=slope_outs, in_specs=[VMEM] * 5 +...  1.69 us
    pallas_call x1, Pallas kernels, per_device(): pl.pallas_call(late_kernel, out_shape=(pltpu.VMEM((2, cells, channels), F...  1.47 us
    all_to_all x1, waiting for transfers between devices, per_device(): lax.all_to_all(sums, 'row', 0, 0, axis_index_groups=[led_by(devices - 1,...  0.87 us
  transfers between devices with their start and end apart: 4, of which 2 were waited for; matrix products, arithmetic and copies ran while one was open for 0% of the time, Pallas kernels for 12%

profile of v4, /device:TPU:0, one launch (start us, length us, event | category | flops | bytes accessed | tf_op | source)
XLA Modules:
  0.0 28.1 jit_solution(4250065248637078115)
XLA Ops:
  0.0 4.4 %reward.1 = (f32[16,4,128]{2,1,0:T(4,128)}, bf16[1,16,16,128]{3,2,1,0:T(8,128)(2,1)S(1)}, bf16[1,16,16,128]{3,2,1,0:T(8,128)(2,1)S(1)}, bf16[3,16,16,128]{3,2,1,...) custom-call(bf16[3,16,48]{2,1,0:T(8,128)(2,1)} %bitcast.7, ...), custom_call_target="tpu_custom_call" | custom-call | tf_op jit(solution)/shard_map/reward/pallas_call | solution.py:605
  4.4 7.9 %all-to-all-start = ((f32[16,4,128]{2,1,0:T(4,128)}), f32[16,4,128]{2,1,0:T(4,128)S(1)}, u32[]{:S(2)}, u32[]{:S(2)}) async-start(f32[16,4,128]{2,1,0:T(4,128)} %get-tuple-element.19), calls=%async_computation | async-start | bytes 65536 | tf_op jit(solution)/shard_map/all_to_all | solution.py:657
  12.3 0.1 collective-permute-start
  12.4 0.7 %collective-permute-start.1 = (bf16[1,16,16,128]{3,2,1,0:T(8,128)(2,1)S(1)}, bf16[1,16,16,128]{3,2,1,0:T(8,128)(2,1)S(1)}, u32[]{:S(2)}, u32[]{:S(2)}) collective-permute-start(bf16[1,16,16,128]{3,2,1,0:T(8,128)(2,1)S(1)} %get-tuple-element.28), channel_id=1, source_target_pairs={{1,2},{3,4},{5,6},{7,8},{9,10},{11,12},{13,14},{2,1},{4,3},{6,5},{... | collective-permute-start | bytes 196616 | tf_op jit(solution)/shard_map/ppermute | solution.py:675
  13.0 0.2 prepare.1.wide
  13.2 2.5 %all-to-all-done.arrived = f32[16,4,128]{2,1,0:T(4,128)S(1)} async-done(((f32[16,4,128]{2,1,0:T(4,128)}), f32[16,4,128]{2,1,0:T(4,128)S(1)}, u32[]{:S(2)}, u32[]{:S(2)}) %all-to-all-start) | async-done | bytes 32800 | tf_op jit(solution)/shard_map/all_to_all | solution.py:657
  15.7 1.7 %slope.1 = (f32[3,256,128]{2,1,0:T(8,128)S(1)}, f32[2,256,128]{2,1,0:T(8,128)S(1)}, f32[8,128]{1,0:T(8,128)S(1)}, f32[16,2,128]{2,1,0:T(2,128)}) custom-call(f32[16,4,128]{2,1,0:T(4,128)S(1)} %all-to-all-done.arrived, bf16[3,16,16,128]{3,2,1,0:T(8,128)(2,1)S(1)} %get-tuple-element.20.hidden, f32[1,128]{1,0:T(1,128)S(1)} %get-tuple-element.21.gain, ...), custom_call_target="tpu_custom_call" | custom-call | tf_op jit(solution)/shard_map/slope/pallas_call | solution.py:658
  17.4 6.4 %all-to-all-start.1 = ((f32[16,2,128]{2,1,0:T(2,128)}), f32[16,2,128]{2,1,0:T(2,128)S(1)}, u32[]{:S(2)}, u32[]{:S(2)}) async-start(f32[16,2,128]{2,1,0:T(2,128)} %get-tuple-element.24), calls=%async_computation.1 | async-start | bytes 32768 | tf_op jit(solution)/shard_map/all_to_all | solution.py:676
  23.7 0.0 collective-permute-done.across
  23.7 0.0 collective-permute-done.1.along
  23.7 1.5 %late.1 = (f32[2,256,128]{2,1,0:T(8,128)S(1)}, bf16[2,16,16,128]{3,2,1,0:T(8,128)(2,1)S(1)}, bf16[1152,384]{1,0:T(8,128)(2,1)S(1)}) custom-call(bf16[1,16,16,128]{3,2,1,0:T(8,128)(2,1)S(1)} %collective-permute-done.across, bf16[1,16,16,128]{3,2,1,0:T(8,128)(2,1)S(1)} %collective-permute-done.1.along, ...), custom_call_target="tpu_custom_call", output_to_operand_aliasing={{0}: (2, {})} | custom-call | tf_op jit(solution)/shard_map/late/pallas_call | solution.py:677
  25.2 0.9 %all-to-all-done.1.arrived = f32[16,2,128]{2,1,0:T(2,128)S(1)} async-done(((f32[16,2,128]{2,1,0:T(2,128)}), f32[16,2,128]{2,1,0:T(2,128)S(1)}, u32[]{:S(2)}, u32[]{:S(2)}) %all-to-all-start.1) | async-done | bytes 16416 | tf_op jit(solution)/shard_map/all_to_all | solution.py:676
  26.1 2.0 %inner.1 = bf16[3,16,16,128]{3,2,1,0:T(8,128)(2,1)} custom-call(f32[16,2,128]{2,1,0:T(2,128)S(1)} %all-to-all-done.1.arrived, f32[8,128]{1,0:T(8,128)S(1)} %get-tuple-element.25.stats, f32[3,256,128]{2,1,0:T(8,128)S(1)} %get-tuple-element.26.direct, bf16[3,16,16,128]{3,2,1,0:T(8,128)(2,1)S(1)} %get-tuple-element.20.hidden, ...), custom_call_target="tpu_custom_call" | custom-call | tf_op jit(solution)/shard_map/inner/pallas_call | solution.py:690
Async XLA Ops:
  4.4 11.3 %all-to-all-start = ((f32[16,4,128]{2,1,0:T(4,128)}), f32[16,4,128]{2,1,0:T(4,128)S(1)}, u32[]{:S(2)}, u32[]{:S(2)}) async-start(f32[16,4,128]{2,1,0:T(4,128)} %get-tuple-element.19), calls=%async_computation | async-start | bytes 65536 | tf_op jit(solution)/shard_map/all_to_all | solution.py:657
  12.3 11.5 %collective-permute-start = (bf16[1,16,16,128]{3,2,1,0:T(8,128)(2,1)S(1)}, bf16[1,16,16,128]{3,2,1,0:T(8,128)(2,1)S(1)}, u32[]{:S(2)}, u32[]{:S(2)}) collective-permute-start(bf16[1,16,16,128]{3,2,1,0:T(8,128)(2,1)S(1)} %get-tuple-element.27), channel_id=1, source_target_pairs={{0,1},{2,3},{4,5},{6,7},{8,9},{10,11},{12,13},{14,15},{1,0},{3,2},... | collective-permute-start | bytes 196616 | tf_op jit(solution)/shard_map/ppermute | solution.py:673
  12.4 11.4 %collective-permute-start.1 = (bf16[1,16,16,128]{3,2,1,0:T(8,128)(2,1)S(1)}, bf16[1,16,16,128]{3,2,1,0:T(8,128)(2,1)S(1)}, u32[]{:S(2)}, u32[]{:S(2)}) collective-permute-start(bf16[1,16,16,128]{3,2,1,0:T(8,128)(2,1)S(1)} %get-tuple-element.28), channel_id=1, source_target_pairs={{1,2},{3,4},{5,6},{7,8},{9,10},{11,12},{13,14},{2,1},{4,3},{6,5},{... | collective-permute-start | bytes 196616 | tf_op jit(solution)/shard_map/ppermute | solution.py:675
  17.4 8.7 %all-to-all-start.1 = ((f32[16,2,128]{2,1,0:T(2,128)}), f32[16,2,128]{2,1,0:T(2,128)S(1)}, u32[]{:S(2)}, u32[]{:S(2)}) async-start(f32[16,2,128]{2,1,0:T(2,128)} %get-tuple-element.24), calls=%async_computation.1 | async-start | bytes 32768 | tf_op jit(solution)/shard_map/all_to_all | solution.py:676

commit v5 on v4

--- a/solution.py
+++ b/solution.py
@@ -58,12 +58,12 @@
 
 
 def exact_rows(rows, product):
-    place = iota((16, rows[0].shape[1]), 0)
+    place = iota((8, rows[0].shape[1]), 0)
     stacked = jnp.zeros(place.shape, F32)
     for index, row in enumerate(rows):
         for step, piece in enumerate(cut_in_three(row)):
             stacked = jnp.where(place == 3 * index + step, piece.astype(F32), stacked)
-    result = product(stacked.astype(BF16))
+    result = product(jnp.concatenate([stacked, jnp.zeros_like(stacked)], axis=0).astype(BF16))
     return [
         result[3 * i : 3 * i + 1] + result[3 * i + 1 : 3 * i + 2] + result[3 * i + 2 : 3 * i + 3]
         for i in range(len(rows))
@@ -103,12 +103,13 @@
     embedded = jnp.zeros((tokens.shape[0], bias.shape[1]), F32)
     for low, high, weight in load_patch():
         embedded = embedded + matmul(tokens[:, low:high], weight)
-    embedded = embedded + bias[...]
+    rows = -(-count // 8) * 8
+    embedded = embedded[:rows] + bias[...]
     centred = embedded - jnp.mean(embedded, axis=1, keepdims=True)
     inv_spread = lax.rsqrt(jnp.mean(centred * centred, axis=1, keepdims=True) + eps_norm)
     normed = centred * inv_spread
     weighted = normed * gain[...]
-    inside = iota((tokens.shape[0], 1), 0) < count
+    inside = iota((rows, 1), 0) < count
     pooled = jnp.sum(jnp.where(inside, weighted, 0.0), axis=0, keepdims=True)
     return normed, inv_spread, pooled
 
@@ -198,7 +199,9 @@
         - jnp.mean(scaled, axis=1, keepdims=True)
         - normed * jnp.mean(scaled * normed, axis=1, keepdims=True)
     )
-    patch_grad = matmul_t(token_grad.astype(BF16), weight[...]).astype(BF16).astype(F32)
+    filler = jnp.zeros((-token_grad.shape[0] % 16, token_grad.shape[1]), F32)
+    token_grad = jnp.concatenate([token_grad, filler], axis=0).astype(BF16)
+    patch_grad = matmul_t(token_grad, weight[...]).astype(BF16).astype(F32)
     write_windows(patch_grad, sums, own_rows, height, send)
 
 
@@ -218,7 +221,7 @@
     sems = refs[-1]
     frames, bias, gain, owner, picks, head_bias, head_out, hidden, _, _, _, patch, head = near
     count += kept
-    depth, depths = 256, (256, 256)
+    depths = (256, 256)
     small = [pltpu.make_async_copy(far[i], near[i], sems.at[i]) for i in range(count)]
     pieces = []
     used = count
@@ -234,12 +237,9 @@
         copy.start()
 
     def load_patch():
-        for low in range(0, patch.shape[0], depth):
-            for copy in pieces[0][low // depths[0] : (low + depth) // depths[0]]:
-                copy.wait()
-            yield low, low + depth, patch[low : low + depth, :]
-        small[1].wait()
-        small[2].wait()
+        for copy in pieces[0] + small[1:3]:
+            copy.wait()
+        yield 0, patch.shape[0], patch[...]
 
     height = frames.shape[2]
     patches = height // PATCH
@@ -616,8 +616,8 @@
         normed, inv_spread, partial = pl.pallas_call(
             forward_kernel,
             out_shape=(
-                jax.ShapeDtypeStruct((token_rows_of(height), width), F32),
-                jax.ShapeDtypeStruct((token_rows_of(height), LANES), F32),
+                jax.ShapeDtypeStruct((-(-count // 8) * 8, width), F32),
+                jax.ShapeDtypeStruct((-(-count // 8) * 8, LANES), F32),
                 jax.ShapeDtypeStruct((1, width), F32),
             ),
             compiler_params=params(cells),

time: 28.4 us -> 28.5 us (level)
  no operation moved by 1% of the time
where the time goes in v5:
time: 28.5 us; the launch traced here: 28.2 us
  starting transfers between devices  15 us (53%)
  Pallas kernels  9.83 us (34%)
  waiting for transfers between devices  3.34 us (12%)
    all_to_all x1, starting transfers between devices, per_device(): lax.all_to_all(send, 'row', 0, 0, axis_index_groups=[first_order(devices)...  7.91 us
    all_to_all x1, starting transfers between devices, per_device(): lax.all_to_all(sums, 'row', 0, 0, axis_index_groups=[led_by(devices - 1,...  6.35 us
    pallas_call x1, Pallas kernels, per_device(): pl.pallas_call(reward_kernel, out_shape=message + tuple((pltpu.VMEM(x.sha...  4.46 us
    all_to_all x1, waiting for transfers between devices, per_device(): lax.all_to_all(send, 'row', 0, 0, axis_index_groups=[first_order(devices)...  2.47 us
    pallas_call x1, Pallas kernels, per_device(): pl.pallas_call(functools.partial(inner_kernel, devices=devices), out_shap...  2.02 us
    pallas_call x1, Pallas kernels, per_device(): pl.pallas_call(slope_kernel, out_shape=slope_outs, in_specs=[VMEM] * 5 +...  1.69 us
    pallas_call x1, Pallas kernels, per_device(): pl.pallas_call(late_kernel, out_shape=(pltpu.VMEM((2, cells, channels), F...  1.47 us
    all_to_all x1, waiting for transfers between devices, per_device(): lax.all_to_all(sums, 'row', 0, 0, axis_index_groups=[led_by(devices - 1,...  0.87 us
  transfers between devices with their start and end apart: 4, of which 2 were waited for; matrix products, arithmetic and copies ran while one was open for 0% of the time, Pallas kernels for 12%

profile of v5, /device:TPU:0, one launch (start us, length us, event | category | flops | bytes accessed | tf_op | source)
XLA Modules:
  0.0 28.2 jit_solution(8022143981322119957)
XLA Ops:
  0.0 4.5 %reward.1 = (f32[16,4,128]{2,1,0:T(4,128)}, bf16[1,16,16,128]{3,2,1,0:T(8,128)(2,1)S(1)}, bf16[1,16,16,128]{3,2,1,0:T(8,128)(2,1)S(1)}, bf16[3,16,16,128]{3,2,1,...) custom-call(bf16[3,16,48]{2,1,0:T(8,128)(2,1)} %bitcast.7, ...), custom_call_target="tpu_custom_call" | custom-call | tf_op jit(solution)/shard_map/reward/pallas_call | solution.py:605
  4.5 7.9 %all-to-all-start = ((f32[16,4,128]{2,1,0:T(4,128)}), f32[16,4,128]{2,1,0:T(4,128)S(1)}, u32[]{:S(2)}, u32[]{:S(2)}) async-start(f32[16,4,128]{2,1,0:T(4,128)} %get-tuple-element.19), calls=%async_computation | async-start | bytes 65536 | tf_op jit(solution)/shard_map/all_to_all | solution.py:657
  12.4 0.1 collective-permute-start
  12.5 0.7 %collective-permute-start.1 = (bf16[1,16,16,128]{3,2,1,0:T(8,128)(2,1)S(1)}, bf16[1,16,16,128]{3,2,1,0:T(8,128)(2,1)S(1)}, u32[]{:S(2)}, u32[]{:S(2)}) collective-permute-start(bf16[1,16,16,128]{3,2,1,0:T(8,128)(2,1)S(1)} %get-tuple-element.28), channel_id=1, source_target_pairs={{1,2},{3,4},{5,6},{7,8},{9,10},{11,12},{13,14},{2,1},{4,3},{6,5},{... | collective-permute-start | bytes 196616 | tf_op jit(solution)/shard_map/ppermute | solution.py:675
  13.1 0.2 prepare.1.wide
  13.3 2.5 %all-to-all-done.arrived = f32[16,4,128]{2,1,0:T(4,128)S(1)} async-done(((f32[16,4,128]{2,1,0:T(4,128)}), f32[16,4,128]{2,1,0:T(4,128)S(1)}, u32[]{:S(2)}, u32[]{:S(2)}) %all-to-all-start) | async-done | bytes 32800 | tf_op jit(solution)/shard_map/all_to_all | solution.py:657
  15.8 1.7 %slope.1 = (f32[3,256,128]{2,1,0:T(8,128)S(1)}, f32[2,256,128]{2,1,0:T(8,128)S(1)}, f32[8,128]{1,0:T(8,128)S(1)}, f32[16,2,128]{2,1,0:T(2,128)}) custom-call(f32[16,4,128]{2,1,0:T(4,128)S(1)} %all-to-all-done.arrived, bf16[3,16,16,128]{3,2,1,0:T(8,128)(2,1)S(1)} %get-tuple-element.20.hidden, f32[1,128]{1,0:T(1,128)S(1)} %get-tuple-element.21.gain, ...), custom_call_target="tpu_custom_call" | custom-call | tf_op jit(solution)/shard_map/slope/pallas_call | solution.py:658
  17.5 6.3 %all-to-all-start.1 = ((f32[16,2,128]{2,1,0:T(2,128)}), f32[16,2,128]{2,1,0:T(2,128)S(1)}, u32[]{:S(2)}, u32[]{:S(2)}) async-start(f32[16,2,128]{2,1,0:T(2,128)} %get-tuple-element.24), calls=%async_computation.1 | async-start | bytes 32768 | tf_op jit(solution)/shard_map/all_to_all | solution.py:676
  23.8 0.0 collective-permute-done.across
  23.8 0.0 collective-permute-done.1.along
  23.8 1.5 %late.1 = (f32[2,256,128]{2,1,0:T(8,128)S(1)}, bf16[2,16,16,128]{3,2,1,0:T(8,128)(2,1)S(1)}, bf16[1152,384]{1,0:T(8,128)(2,1)S(1)}) custom-call(bf16[1,16,16,128]{3,2,1,0:T(8,128)(2,1)S(1)} %collective-permute-done.across, bf16[1,16,16,128]{3,2,1,0:T(8,128)(2,1)S(1)} %collective-permute-done.1.along, ...), custom_call_target="tpu_custom_call", output_to_operand_aliasing={{0}: (2, {})} | custom-call | tf_op jit(solution)/shard_map/late/pallas_call | solution.py:677
  25.3 0.9 %all-to-all-done.1.arrived = f32[16,2,128]{2,1,0:T(2,128)S(1)} async-done(((f32[16,2,128]{2,1,0:T(2,128)}), f32[16,2,128]{2,1,0:T(2,128)S(1)}, u32[]{:S(2)}, u32[]{:S(2)}) %all-to-all-start.1) | async-done | bytes 16416 | tf_op jit(solution)/shard_map/all_to_all | solution.py:676
  26.2 2.0 %inner.1 = bf16[3,16,16,128]{3,2,1,0:T(8,128)(2,1)} custom-call(f32[16,2,128]{2,1,0:T(2,128)S(1)} %all-to-all-done.1.arrived, f32[8,128]{1,0:T(8,128)S(1)} %get-tuple-element.25.stats, f32[3,256,128]{2,1,0:T(8,128)S(1)} %get-tuple-element.26.direct, bf16[3,16,16,128]{3,2,1,0:T(8,128)(2,1)S(1)} %get-tuple-element.20.hidden, ...), custom_call_target="tpu_custom_call" | custom-call | tf_op jit(solution)/shard_map/inner/pallas_call | solution.py:690
Async XLA Ops:
  4.5 11.3 %all-to-all-start = ((f32[16,4,128]{2,1,0:T(4,128)}), f32[16,4,128]{2,1,0:T(4,128)S(1)}, u32[]{:S(2)}, u32[]{:S(2)}) async-start(f32[16,4,128]{2,1,0:T(4,128)} %get-tuple-element.19), calls=%async_computation | async-start | bytes 65536 | tf_op jit(solution)/shard_map/all_to_all | solution.py:657
  12.4 11.5 %collective-permute-start = (bf16[1,16,16,128]{3,2,1,0:T(8,128)(2,1)S(1)}, bf16[1,16,16,128]{3,2,1,0:T(8,128)(2,1)S(1)}, u32[]{:S(2)}, u32[]{:S(2)}) collective-permute-start(bf16[1,16,16,128]{3,2,1,0:T(8,128)(2,1)S(1)} %get-tuple-element.27), channel_id=1, source_target_pairs={{0,1},{2,3},{4,5},{6,7},{8,9},{10,11},{12,13},{14,15},{1,0},{3,2},... | collective-permute-start | bytes 196616 | tf_op jit(solution)/shard_map/ppermute | solution.py:673
  12.5 11.4 %collective-permute-start.1 = (bf16[1,16,16,128]{3,2,1,0:T(8,128)(2,1)S(1)}, bf16[1,16,16,128]{3,2,1,0:T(8,128)(2,1)S(1)}, u32[]{:S(2)}, u32[]{:S(2)}) collective-permute-start(bf16[1,16,16,128]{3,2,1,0:T(8,128)(2,1)S(1)} %get-tuple-element.28), channel_id=1, source_target_pairs={{1,2},{3,4},{5,6},{7,8},{9,10},{11,12},{13,14},{2,1},{4,3},{6,5},{... | collective-permute-start | bytes 196616 | tf_op jit(solution)/shard_map/ppermute | solution.py:675
  17.5 8.7 %all-to-all-start.1 = ((f32[16,2,128]{2,1,0:T(2,128)}), f32[16,2,128]{2,1,0:T(2,128)S(1)}, u32[]{:S(2)}, u32[]{:S(2)}) async-start(f32[16,2,128]{2,1,0:T(2,128)} %get-tuple-element.24), calls=%async_computation.1 | async-start | bytes 32768 | tf_op jit(solution)/shard_map/all_to_all | solution.py:676

commit v6 on v5

--- a/solution.py
+++ b/solution.py
@@ -504,7 +504,7 @@
 
 
 def inner_kernel(
-    arrived, stats, direct, hidden, edge_direct, edge_states, turned, far_out, padded, out, sems, *, devices
+    arrived, stats, direct, hidden, edge_direct, edge_states, turned, far_out, out, sems, *, devices
 ):
     own_rows, frame_count, width, channels = out.shape
     cells = frame_count * width
@@ -520,6 +520,8 @@
     factor = second / cell_total * inverse * inverse
     position = lax.axis_index("row")
     in_frame = mod(iota((cells, 1), 0), width)
+    results = [jnp.zeros((cells, channels), F32) for _ in range(own_rows)]
+    copies = []
     for i in range(own_rows + 2):
         if 0 < i < own_rows + 1:
             state, part = hidden[i - 1], direct[i - 1]
@@ -532,19 +534,16 @@
             grad = jnp.where(position < devices - 1, grad, 0.0)
         after = jnp.where(in_frame < width - 1, pltpu.roll(grad, cells - 1, 0), 0.0)
         prior = jnp.where(in_frame > 0, pltpu.roll(grad, 1, 0), 0.0)
-        padded[i, :cells, 0:channels] = after.astype(BF16)
-        padded[i, :cells, channels : 2 * channels] = grad.astype(BF16)
-        padded[i, :cells, 2 * channels :] = prior.astype(BF16)
-        padded[i, cells:, :] = jnp.zeros((2 * width, 3 * channels), BF16)
-    results = [jnp.zeros((cells, channels), F32) for _ in range(own_rows)]
-    copies = []
-    for i in range(own_rows + 2):
-        joined = jnp.concatenate(
-            [padded[i, (2 - a) * width : (2 - a) * width + cells, :] for a in range(3)], axis=1
-        )
-        taps = [b for b in range(3) if 0 <= i + b - 2 < own_rows]
-        for low in range(0, len(taps), 2):
-            some = taps[low : low + 2]
+        taps = jnp.concatenate([after.astype(BF16), grad.astype(BF16), prior.astype(BF16)], axis=1)
+        later = []
+        for a in range(3):
+            skip = (2 - a) * width
+            filler = jnp.zeros((skip, taps.shape[1]), BF16)
+            later.append(jnp.concatenate([taps[skip:], filler], axis=0) if skip else taps)
+        joined = jnp.concatenate(later, axis=1)
+        rows = [b for b in range(3) if 0 <= i + b - 2 < own_rows]
+        for low in range(0, len(rows), 2):
+            some = rows[low : low + 2]
             product = matmul(joined, turned[:, some[0] * channels : (some[-1] + 1) * channels])
             for step, b in enumerate(some):
                 results[i + b - 2] = results[i + b - 2] + product[:, step * channels : (step + 1) * channels]
@@ -693,7 +692,6 @@
         in_specs=[VMEM] * 7,
         out_specs=FAR,
         scratch_shapes=[
-            pltpu.VMEM((own_rows + 2, cells + 2 * frame_width, 3 * channels), BF16),
             pltpu.VMEM(hidden_state.shape, BF16),
             pltpu.SemaphoreType.DMA((own_rows,)),
         ],

time: 28.5 us -> 28.4 us (level)
  no operation moved by 1% of the time
where the time goes in v6:
time: 28.4 us; the launch traced here: 28.2 us
  starting transfers between devices  15 us (53%)
  Pallas kernels  9.77 us (34%)
  waiting for transfers between devices  3.34 us (12%)
    all_to_all x1, starting transfers between devices, per_device(): lax.all_to_all(send, 'row', 0, 0, axis_index_groups=[first_order(devices)...  7.91 us
    all_to_all x1, starting transfers between devices, per_device(): lax.all_to_all(sums, 'row', 0, 0, axis_index_groups=[led_by(devices - 1,...  6.35 us
    pallas_call x1, Pallas kernels, per_device(): pl.pallas_call(reward_kernel, out_shape=message + tuple((pltpu.VMEM(x.sha...  4.46 us
    all_to_all x1, waiting for transfers between devices, per_device(): lax.all_to_all(send, 'row', 0, 0, axis_index_groups=[first_order(devices)...  2.47 us
    pallas_call x1, Pallas kernels, per_device(): pl.pallas_call(functools.partial(inner_kernel, devices=devices), out_shap...  1.96 us
    pallas_call x1, Pallas kernels, per_device(): pl.pallas_call(slope_kernel, out_shape=slope_outs, in_specs=[VMEM] * 5 +...  1.69 us
    pallas_call x1, Pallas kernels, per_device(): pl.pallas_call(late_kernel, out_shape=(pltpu.VMEM((2, cells, channels), F...  1.47 us
    all_to_all x1, waiting for transfers between devices, per_device(): lax.all_to_all(sums, 'row', 0, 0, axis_index_groups=[led_by(devices - 1,...  0.87 us
  transfers between devices with their start and end apart: 4, of which 2 were waited for; matrix products, arithmetic and copies ran while one was open for 0% of the time, Pallas kernels for 12%

profile of v6, /device:TPU:0, one launch (start us, length us, event | category | flops | bytes accessed | tf_op | source)
XLA Modules:
  0.0 28.2 jit_solution(9019081121429313939)
XLA Ops:
  0.0 4.5 %reward.1 = (f32[16,4,128]{2,1,0:T(4,128)}, bf16[1,16,16,128]{3,2,1,0:T(8,128)(2,1)S(1)}, bf16[1,16,16,128]{3,2,1,0:T(8,128)(2,1)S(1)}, bf16[3,16,16,128]{3,2,1,...) custom-call(bf16[3,16,48]{2,1,0:T(8,128)(2,1)} %bitcast.7, ...), custom_call_target="tpu_custom_call" | custom-call | tf_op jit(solution)/shard_map/reward/pallas_call | solution.py:604
  4.5 7.9 %all-to-all-start = ((f32[16,4,128]{2,1,0:T(4,128)}), f32[16,4,128]{2,1,0:T(4,128)S(1)}, u32[]{:S(2)}, u32[]{:S(2)}) async-start(f32[16,4,128]{2,1,0:T(4,128)} %get-tuple-element.19), calls=%async_computation | async-start | bytes 65536 | tf_op jit(solution)/shard_map/all_to_all | solution.py:656
  12.4 0.1 collective-permute-start
  12.5 0.7 %collective-permute-start.1 = (bf16[1,16,16,128]{3,2,1,0:T(8,128)(2,1)S(1)}, bf16[1,16,16,128]{3,2,1,0:T(8,128)(2,1)S(1)}, u32[]{:S(2)}, u32[]{:S(2)}) collective-permute-start(bf16[1,16,16,128]{3,2,1,0:T(8,128)(2,1)S(1)} %get-tuple-element.28), channel_id=1, source_target_pairs={{1,2},{3,4},{5,6},{7,8},{9,10},{11,12},{13,14},{2,1},{4,3},{6,5},{... | collective-permute-start | bytes 196616 | tf_op jit(solution)/shard_map/ppermute | solution.py:674
  13.1 0.2 prepare.1.wide
  13.3 2.5 %all-to-all-done.arrived = f32[16,4,128]{2,1,0:T(4,128)S(1)} async-done(((f32[16,4,128]{2,1,0:T(4,128)}), f32[16,4,128]{2,1,0:T(4,128)S(1)}, u32[]{:S(2)}, u32[]{:S(2)}) %all-to-all-start) | async-done | bytes 32800 | tf_op jit(solution)/shard_map/all_to_all | solution.py:656
  15.8 1.7 %slope.1 = (f32[3,256,128]{2,1,0:T(8,128)S(1)}, f32[2,256,128]{2,1,0:T(8,128)S(1)}, f32[8,128]{1,0:T(8,128)S(1)}, f32[16,2,128]{2,1,0:T(2,128)}) custom-call(f32[16,4,128]{2,1,0:T(4,128)S(1)} %all-to-all-done.arrived, bf16[3,16,16,128]{3,2,1,0:T(8,128)(2,1)S(1)} %get-tuple-element.20.hidden, f32[1,128]{1,0:T(1,128)S(1)} %get-tuple-element.21.gain, ...), custom_call_target="tpu_custom_call" | custom-call | tf_op jit(solution)/shard_map/slope/pallas_call | solution.py:657
  17.5 6.3 %all-to-all-start.1 = ((f32[16,2,128]{2,1,0:T(2,128)}), f32[16,2,128]{2,1,0:T(2,128)S(1)}, u32[]{:S(2)}, u32[]{:S(2)}) async-start(f32[16,2,128]{2,1,0:T(2,128)} %get-tuple-element.24), calls=%async_computation.1 | async-start | bytes 32768 | tf_op jit(solution)/shard_map/all_to_all | solution.py:675
  23.8 0.0 collective-permute-done.across
  23.8 0.0 collective-permute-done.1.along
  23.8 1.5 %late.1 = (f32[2,256,128]{2,1,0:T(8,128)S(1)}, bf16[2,16,16,128]{3,2,1,0:T(8,128)(2,1)S(1)}, bf16[1152,384]{1,0:T(8,128)(2,1)S(1)}) custom-call(bf16[1,16,16,128]{3,2,1,0:T(8,128)(2,1)S(1)} %collective-permute-done.across, bf16[1,16,16,128]{3,2,1,0:T(8,128)(2,1)S(1)} %collective-permute-done.1.along, ...), custom_call_target="tpu_custom_call", output_to_operand_aliasing={{0}: (2, {})} | custom-call | tf_op jit(solution)/shard_map/late/pallas_call | solution.py:676
  25.3 0.9 %all-to-all-done.1.arrived = f32[16,2,128]{2,1,0:T(2,128)S(1)} async-done(((f32[16,2,128]{2,1,0:T(2,128)}), f32[16,2,128]{2,1,0:T(2,128)S(1)}, u32[]{:S(2)}, u32[]{:S(2)}) %all-to-all-start.1) | async-done | bytes 16416 | tf_op jit(solution)/shard_map/all_to_all | solution.py:675
  26.2 2.0 %inner.1 = bf16[3,16,16,128]{3,2,1,0:T(8,128)(2,1)} custom-call(f32[16,2,128]{2,1,0:T(2,128)S(1)} %all-to-all-done.1.arrived, f32[8,128]{1,0:T(8,128)S(1)} %get-tuple-element.25.stats, f32[3,256,128]{2,1,0:T(8,128)S(1)} %get-tuple-element.26.direct, bf16[3,16,16,128]{3,2,1,0:T(8,128)(2,1)S(1)} %get-tuple-element.20.hidden, ...), custom_call_target="tpu_custom_call" | custom-call | tf_op jit(solution)/shard_map/inner/pallas_call | solution.py:689
Async XLA Ops:
  4.5 11.3 %all-to-all-start = ((f32[16,4,128]{2,1,0:T(4,128)}), f32[16,4,128]{2,1,0:T(4,128)S(1)}, u32[]{:S(2)}, u32[]{:S(2)}) async-start(f32[16,4,128]{2,1,0:T(4,128)} %get-tuple-element.19), calls=%async_computation | async-start | bytes 65536 | tf_op jit(solution)/shard_map/all_to_all | solution.py:656
  12.4 11.5 %collective-permute-start = (bf16[1,16,16,128]{3,2,1,0:T(8,128)(2,1)S(1)}, bf16[1,16,16,128]{3,2,1,0:T(8,128)(2,1)S(1)}, u32[]{:S(2)}, u32[]{:S(2)}) collective-permute-start(bf16[1,16,16,128]{3,2,1,0:T(8,128)(2,1)S(1)} %get-tuple-element.27), channel_id=1, source_target_pairs={{0,1},{2,3},{4,5},{6,7},{8,9},{10,11},{12,13},{14,15},{1,0},{3,2},... | collective-permute-start | bytes 196616 | tf_op jit(solution)/shard_map/ppermute | solution.py:672
  12.5 11.4 %collective-permute-start.1 = (bf16[1,16,16,128]{3,2,1,0:T(8,128)(2,1)S(1)}, bf16[1,16,16,128]{3,2,1,0:T(8,128)(2,1)S(1)}, u32[]{:S(2)}, u32[]{:S(2)}) collective-permute-start(bf16[1,16,16,128]{3,2,1,0:T(8,128)(2,1)S(1)} %get-tuple-element.28), channel_id=1, source_target_pairs={{1,2},{3,4},{5,6},{7,8},{9,10},{11,12},{13,14},{2,1},{4,3},{6,5},{... | collective-permute-start | bytes 196616 | tf_op jit(solution)/shard_map/ppermute | solution.py:674
  17.5 8.7 %all-to-all-start.1 = ((f32[16,2,128]{2,1,0:T(2,128)}), f32[16,2,128]{2,1,0:T(2,128)S(1)}, u32[]{:S(2)}, u32[]{:S(2)}) async-start(f32[16,2,128]{2,1,0:T(2,128)} %get-tuple-element.24), calls=%async_computation.1 | async-start | bytes 32768 | tf_op jit(solution)/shard_map/all_to_all | solution.py:675

commit v7 on v6

--- a/solution.py
+++ b/solution.py
@@ -233,7 +233,13 @@
             parts.append(pltpu.make_async_copy(source.at[part], target.at[part], sems.at[used]))
             used += 1
         pieces.append(parts)
-    for copy in [small[0], small[7]] + pieces[0] + small[1:7] + pieces[1] + small[8:]:
+    last = hidden.shape[0] - 1
+    even = position % 2 == 0
+    edges = [
+        pltpu.make_async_copy(far[7].at[pl.ds(jnp.where(even, last, 0), 1)], across, sems.at[used]),
+        pltpu.make_async_copy(far[7].at[pl.ds(jnp.where(even, 0, last), 1)], along, sems.at[used + 1]),
+    ]
+    for copy in [small[0]] + pieces[0] + small[1:7] + pieces[1] + small[7:] + edges:
         copy.start()
 
     def load_patch():
@@ -244,12 +250,9 @@
     height = frames.shape[2]
     patches = height // PATCH
     small[0].wait()
-    small[7].wait()
     tokens = to_tokens(frames[...])
-    sums = group_sums(hidden[...])
-    write_edges(position, hidden, across, along)
     normed, inv_spread, pooled = forward_part(tokens, patches, bias, gain, load_patch)
-    for copy in small[3:7]:
+    for copy in small[3:8]:
         copy.wait()
 
     def through_head(rows):
@@ -274,10 +277,10 @@
         position,
         hidden.shape[0],
         height,
-        sums,
+        group_sums(hidden[...]),
         send,
     )
-    for copy in small[8:]:
+    for copy in small[8:] + edges:
         copy.wait()
 
 

time: 28.4 us -> 28.8 us (1.014)
  Pallas kernels: 9.77 us -> 10.1 us
    pallas_call x1, Pallas kernels: 4.46 us -> 4.81 us  [per_device(): pl.pallas_call(reward_kernel, out_shape=message + tuple((pltpu.VMEM(x.sha...]
where the time goes in v7:
time: 28.8 us; the launch traced here: 28.5 us
  starting transfers between devices  15 us (52%)
  Pallas kernels  10.1 us (35%)
  waiting for transfers between devices  3.34 us (12%)
    all_to_all x1, starting transfers between devices, per_device(): lax.all_to_all(send, 'row', 0, 0, axis_index_groups=[first_order(devices)...  7.91 us
    all_to_all x1, starting transfers between devices, per_device(): lax.all_to_all(sums, 'row', 0, 0, axis_index_groups=[led_by(devices - 1,...  6.36 us
    pallas_call x1, Pallas kernels, per_device(): pl.pallas_call(reward_kernel, out_shape=message + tuple((pltpu.VMEM(x.sha...  4.81 us
    all_to_all x1, waiting for transfers between devices, per_device(): lax.all_to_all(send, 'row', 0, 0, axis_index_groups=[first_order(devices)...  2.47 us
    pallas_call x1, Pallas kernels, per_device(): pl.pallas_call(functools.partial(inner_kernel, devices=devices), out_shap...  1.96 us
    pallas_call x1, Pallas kernels, per_device(): pl.pallas_call(slope_kernel, out_shape=slope_outs, in_specs=[VMEM] * 5 +...  1.69 us
    pallas_call x1, Pallas kernels, per_device(): pl.pallas_call(late_kernel, out_shape=(pltpu.VMEM((2, cells, channels), F...  1.47 us
    all_to_all x1, waiting for transfers between devices, per_device(): lax.all_to_all(sums, 'row', 0, 0, axis_index_groups=[led_by(devices - 1,...  0.87 us
  transfers between devices with their start and end apart: 4, of which 2 were waited for; matrix products, arithmetic and copies ran while one was open for 0% of the time, Pallas kernels for 12%

profile of v7, /device:TPU:0, one launch (start us, length us, event | category | flops | bytes accessed | tf_op | source)
XLA Modules:
  0.0 28.5 jit_solution(8116792068938107345)
XLA Ops:
  0.0 4.8 %reward.1 = (f32[16,4,128]{2,1,0:T(4,128)}, bf16[1,16,16,128]{3,2,1,0:T(8,128)(2,1)S(1)}, bf16[1,16,16,128]{3,2,1,0:T(8,128)(2,1)S(1)}, bf16[3,16,16,128]{3,2,1,...) custom-call(bf16[3,16,48]{2,1,0:T(8,128)(2,1)} %bitcast.7, ...), custom_call_target="tpu_custom_call" | custom-call | tf_op jit(solution)/shard_map/reward/pallas_call | solution.py:607
  4.8 7.9 %all-to-all-start = ((f32[16,4,128]{2,1,0:T(4,128)}), f32[16,4,128]{2,1,0:T(4,128)S(1)}, u32[]{:S(2)}, u32[]{:S(2)}) async-start(f32[16,4,128]{2,1,0:T(4,128)} %get-tuple-element.19), calls=%async_computation | async-start | bytes 65536 | tf_op jit(solution)/shard_map/all_to_all | solution.py:659
  12.7 0.1 collective-permute-start
  12.8 0.7 %collective-permute-start.1 = (bf16[1,16,16,128]{3,2,1,0:T(8,128)(2,1)S(1)}, bf16[1,16,16,128]{3,2,1,0:T(8,128)(2,1)S(1)}, u32[]{:S(2)}, u32[]{:S(2)}) collective-permute-start(bf16[1,16,16,128]{3,2,1,0:T(8,128)(2,1)S(1)} %get-tuple-element.28), channel_id=1, source_target_pairs={{1,2},{3,4},{5,6},{7,8},{9,10},{11,12},{13,14},{2,1},{4,3},{6,5},{... | collective-permute-start | bytes 196616 | tf_op jit(solution)/shard_map/ppermute | solution.py:677
  13.5 0.2 prepare.1.wide
  13.7 2.5 %all-to-all-done.arrived = f32[16,4,128]{2,1,0:T(4,128)S(1)} async-done(((f32[16,4,128]{2,1,0:T(4,128)}), f32[16,4,128]{2,1,0:T(4,128)S(1)}, u32[]{:S(2)}, u32[]{:S(2)}) %all-to-all-start) | async-done | bytes 32800 | tf_op jit(solution)/shard_map/all_to_all | solution.py:659
  16.1 1.7 %slope.1 = (f32[3,256,128]{2,1,0:T(8,128)S(1)}, f32[2,256,128]{2,1,0:T(8,128)S(1)}, f32[8,128]{1,0:T(8,128)S(1)}, f32[16,2,128]{2,1,0:T(2,128)}) custom-call(f32[16,4,128]{2,1,0:T(4,128)S(1)} %all-to-all-done.arrived, bf16[3,16,16,128]{3,2,1,0:T(8,128)(2,1)S(1)} %get-tuple-element.20.hidden, f32[1,128]{1,0:T(1,128)S(1)} %get-tuple-element.21.gain, ...), custom_call_target="tpu_custom_call" | custom-call | tf_op jit(solution)/shard_map/slope/pallas_call | solution.py:660
  17.8 6.4 %all-to-all-start.1 = ((f32[16,2,128]{2,1,0:T(2,128)}), f32[16,2,128]{2,1,0:T(2,128)S(1)}, u32[]{:S(2)}, u32[]{:S(2)}) async-start(f32[16,2,128]{2,1,0:T(2,128)} %get-tuple-element.24), calls=%async_computation.1 | async-start | bytes 32768 | tf_op jit(solution)/shard_map/all_to_all | solution.py:678
  24.2 0.0 collective-permute-done.across
  24.2 0.0 collective-permute-done.1.along
  24.2 1.5 %late.1 = (f32[2,256,128]{2,1,0:T(8,128)S(1)}, bf16[2,16,16,128]{3,2,1,0:T(8,128)(2,1)S(1)}, bf16[1152,384]{1,0:T(8,128)(2,1)S(1)}) custom-call(bf16[1,16,16,128]{3,2,1,0:T(8,128)(2,1)S(1)} %collective-permute-done.across, bf16[1,16,16,128]{3,2,1,0:T(8,128)(2,1)S(1)} %collective-permute-done.1.along, ...), custom_call_target="tpu_custom_call", output_to_operand_aliasing={{0}: (2, {})} | custom-call | tf_op jit(solution)/shard_map/late/pallas_call | solution.py:679
  25.7 0.9 %all-to-all-done.1.arrived = f32[16,2,128]{2,1,0:T(2,128)S(1)} async-done(((f32[16,2,128]{2,1,0:T(2,128)}), f32[16,2,128]{2,1,0:T(2,128)S(1)}, u32[]{:S(2)}, u32[]{:S(2)}) %all-to-all-start.1) | async-done | bytes 16416 | tf_op jit(solution)/shard_map/all_to_all | solution.py:678
  26.5 2.0 %inner.1 = bf16[3,16,16,128]{3,2,1,0:T(8,128)(2,1)} custom-call(f32[16,2,128]{2,1,0:T(2,128)S(1)} %all-to-all-done.1.arrived, f32[8,128]{1,0:T(8,128)S(1)} %get-tuple-element.25.stats, f32[3,256,128]{2,1,0:T(8,128)S(1)} %get-tuple-element.26.direct, bf16[3,16,16,128]{3,2,1,0:T(8,128)(2,1)S(1)} %get-tuple-element.20.hidden, ...), custom_call_target="tpu_custom_call" | custom-call | tf_op jit(solution)/shard_map/inner/pallas_call | solution.py:692
Async XLA Ops:
  4.8 11.3 %all-to-all-start = ((f32[16,4,128]{2,1,0:T(4,128)}), f32[16,4,128]{2,1,0:T(4,128)S(1)}, u32[]{:S(2)}, u32[]{:S(2)}) async-start(f32[16,4,128]{2,1,0:T(4,128)} %get-tuple-element.19), calls=%async_computation | async-start | bytes 65536 | tf_op jit(solution)/shard_map/all_to_all | solution.py:659
  12.7 11.5 %collective-permute-start = (bf16[1,16,16,128]{3,2,1,0:T(8,128)(2,1)S(1)}, bf16[1,16,16,128]{3,2,1,0:T(8,128)(2,1)S(1)}, u32[]{:S(2)}, u32[]{:S(2)}) collective-permute-start(bf16[1,16,16,128]{3,2,1,0:T(8,128)(2,1)S(1)} %get-tuple-element.27), channel_id=1, source_target_pairs={{0,1},{2,3},{4,5},{6,7},{8,9},{10,11},{12,13},{14,15},{1,0},{3,2},... | collective-permute-start | bytes 196616 | tf_op jit(solution)/shard_map/ppermute | solution.py:675
  12.8 11.4 %collective-permute-start.1 = (bf16[1,16,16,128]{3,2,1,0:T(8,128)(2,1)S(1)}, bf16[1,16,16,128]{3,2,1,0:T(8,128)(2,1)S(1)}, u32[]{:S(2)}, u32[]{:S(2)}) collective-permute-start(bf16[1,16,16,128]{3,2,1,0:T(8,128)(2,1)S(1)} %get-tuple-element.28), channel_id=1, source_target_pairs={{1,2},{3,4},{5,6},{7,8},{9,10},{11,12},{13,14},{2,1},{4,3},{6,5},{... | collective-permute-start | bytes 196616 | tf_op jit(solution)/shard_map/ppermute | solution.py:677
  17.8 8.7 %all-to-all-start.1 = ((f32[16,2,128]{2,1,0:T(2,128)}), f32[16,2,128]{2,1,0:T(2,128)S(1)}, u32[]{:S(2)}, u32[]{:S(2)}) async-start(f32[16,2,128]{2,1,0:T(2,128)} %get-tuple-element.24), calls=%async_computation.1 | async-start | bytes 32768 | tf_op jit(solution)/shard_map/all_to_all | solution.py:678

commit v8 on v6

--- a/solution.py
+++ b/solution.py
@@ -371,9 +371,9 @@
     return mean, lax.rsqrt(second / cell_total - mean * mean + eps_norm)
 
 
-def norm_slopes(state, mean, inverse, gain, shift):
-    normed = (state - mean) * inverse
-    return normed, silu_slope(normed * gain + shift) * gain
+def scaled_slopes(state, mean, inverse, gain, shift):
+    scale = gain * inverse
+    return silu_slope(state * scale + (shift - mean * scale)) * scale
 
 
 def slope_kernel(
@@ -405,7 +405,7 @@
     mean, inverse = norm_constants(totals, own_rows * devices * cells * (channels // GROUPS))
     for i in range(own_rows):
         state = hidden[i].reshape(cells, channels).astype(F32)
-        slopes_own[i] = norm_slopes(state, mean, inverse, gain[...], shift[...])[1] * inverse
+        slopes_own[i] = scaled_slopes(state, mean, inverse, gain[...], shift[...])
 
     if per_frame == 1:
         lane = iota((1, LANES), 1)
@@ -493,7 +493,7 @@
         state = jnp.where(odd == (i == 0), across[0], along[0])
         states[i] = state
         values = state.reshape(cells, channels).astype(F32)
-        direct[i] = slopes[i] * norm_slopes(values, mean, inverse, gain[...], shift[...])[1] * inverse
+        direct[i] = slopes[i] * scaled_slopes(values, mean, inverse, gain[...], shift[...])
     copy.wait()
     size = inner_weight.shape[3]
     for b in range(3):

time: 28.4 us -> 28.5 us (level)
  no operation moved by 1% of the time
where the time goes in v8:
time: 28.5 us; the launch traced here: 28.2 us
  starting transfers between devices  15 us (53%)
  Pallas kernels  9.78 us (34%)
  waiting for transfers between devices  3.34 us (12%)
    all_to_all x1, starting transfers between devices, per_device(): lax.all_to_all(send, 'row', 0, 0, axis_index_groups=[first_order(devices)...  7.91 us
    all_to_all x1, starting transfers between devices, per_device(): lax.all_to_all(sums, 'row', 0, 0, axis_index_groups=[led_by(devices - 1,...  6.35 us
    pallas_call x1, Pallas kernels, per_device(): pl.pallas_call(reward_kernel, out_shape=message + tuple((pltpu.VMEM(x.sha...  4.46 us
    all_to_all x1, waiting for transfers between devices, per_device(): lax.all_to_all(send, 'row', 0, 0, axis_index_groups=[first_order(devices)...  2.47 us
    pallas_call x1, Pallas kernels, per_device(): pl.pallas_call(functools.partial(inner_kernel, devices=devices), out_shap...  1.96 us
    pallas_call x1, Pallas kernels, per_device(): pl.pallas_call(slope_kernel, out_shape=slope_outs, in_specs=[VMEM] * 5 +...  1.71 us
    pallas_call x1, Pallas kernels, per_device(): pl.pallas_call(late_kernel, out_shape=(pltpu.VMEM((2, cells, channels), F...  1.47 us
    all_to_all x1, waiting for transfers between devices, per_device(): lax.all_to_all(sums, 'row', 0, 0, axis_index_groups=[led_by(devices - 1,...  0.87 us
  transfers between devices with their start and end apart: 4, of which 2 were waited for; matrix products, arithmetic and copies ran while one was open for 0% of the time, Pallas kernels for 12%

profile of v8, /device:TPU:0, one launch (start us, length us, event | category | flops | bytes accessed | tf_op | source)
XLA Modules:
  0.0 28.2 jit_solution(813299723228957945)
XLA Ops:
  0.0 4.5 %reward.1 = (f32[16,4,128]{2,1,0:T(4,128)}, bf16[1,16,16,128]{3,2,1,0:T(8,128)(2,1)S(1)}, bf16[1,16,16,128]{3,2,1,0:T(8,128)(2,1)S(1)}, bf16[3,16,16,128]{3,2,1,...) custom-call(bf16[3,16,48]{2,1,0:T(8,128)(2,1)} %bitcast.7, ...), custom_call_target="tpu_custom_call" | custom-call | tf_op jit(solution)/shard_map/reward/pallas_call | solution.py:604
  4.5 7.9 %all-to-all-start = ((f32[16,4,128]{2,1,0:T(4,128)}), f32[16,4,128]{2,1,0:T(4,128)S(1)}, u32[]{:S(2)}, u32[]{:S(2)}) async-start(f32[16,4,128]{2,1,0:T(4,128)} %get-tuple-element.19), calls=%async_computation | async-start | bytes 65536 | tf_op jit(solution)/shard_map/all_to_all | solution.py:656
  12.4 0.1 collective-permute-start
  12.5 0.7 %collective-permute-start.1 = (bf16[1,16,16,128]{3,2,1,0:T(8,128)(2,1)S(1)}, bf16[1,16,16,128]{3,2,1,0:T(8,128)(2,1)S(1)}, u32[]{:S(2)}, u32[]{:S(2)}) collective-permute-start(bf16[1,16,16,128]{3,2,1,0:T(8,128)(2,1)S(1)} %get-tuple-element.28), channel_id=1, source_target_pairs={{1,2},{3,4},{5,6},{7,8},{9,10},{11,12},{13,14},{2,1},{4,3},{6,5},{... | collective-permute-start | bytes 196616 | tf_op jit(solution)/shard_map/ppermute | solution.py:674
  13.1 0.2 prepare.1.wide
  13.3 2.5 %all-to-all-done.arrived = f32[16,4,128]{2,1,0:T(4,128)S(1)} async-done(((f32[16,4,128]{2,1,0:T(4,128)}), f32[16,4,128]{2,1,0:T(4,128)S(1)}, u32[]{:S(2)}, u32[]{:S(2)}) %all-to-all-start) | async-done | bytes 32800 | tf_op jit(solution)/shard_map/all_to_all | solution.py:656
  15.8 1.7 %slope.1 = (f32[3,256,128]{2,1,0:T(8,128)S(1)}, f32[2,256,128]{2,1,0:T(8,128)S(1)}, f32[8,128]{1,0:T(8,128)S(1)}, f32[16,2,128]{2,1,0:T(2,128)}) custom-call(f32[16,4,128]{2,1,0:T(4,128)S(1)} %all-to-all-done.arrived, bf16[3,16,16,128]{3,2,1,0:T(8,128)(2,1)S(1)} %get-tuple-element.20.hidden, f32[1,128]{1,0:T(1,128)S(1)} %get-tuple-element.21.gain, ...), custom_call_target="tpu_custom_call" | custom-call | tf_op jit(solution)/shard_map/slope/pallas_call | solution.py:657
  17.5 6.4 %all-to-all-start.1 = ((f32[16,2,128]{2,1,0:T(2,128)}), f32[16,2,128]{2,1,0:T(2,128)S(1)}, u32[]{:S(2)}, u32[]{:S(2)}) async-start(f32[16,2,128]{2,1,0:T(2,128)} %get-tuple-element.24), calls=%async_computation.1 | async-start | bytes 32768 | tf_op jit(solution)/shard_map/all_to_all | solution.py:675
  23.8 0.0 collective-permute-done.across
  23.9 0.0 collective-permute-done.1.along
  23.9 1.5 %late.1 = (f32[2,256,128]{2,1,0:T(8,128)S(1)}, bf16[2,16,16,128]{3,2,1,0:T(8,128)(2,1)S(1)}, bf16[1152,384]{1,0:T(8,128)(2,1)S(1)}) custom-call(bf16[1,16,16,128]{3,2,1,0:T(8,128)(2,1)S(1)} %collective-permute-done.across, bf16[1,16,16,128]{3,2,1,0:T(8,128)(2,1)S(1)} %collective-permute-done.1.along, ...), custom_call_target="tpu_custom_call", output_to_operand_aliasing={{0}: (2, {})} | custom-call | tf_op jit(solution)/shard_map/late/pallas_call | solution.py:676
  25.3 0.9 %all-to-all-done.1.arrived = f32[16,2,128]{2,1,0:T(2,128)S(1)} async-done(((f32[16,2,128]{2,1,0:T(2,128)}), f32[16,2,128]{2,1,0:T(2,128)S(1)}, u32[]{:S(2)}, u32[]{:S(2)}) %all-to-all-start.1) | async-done | bytes 16416 | tf_op jit(solution)/shard_map/all_to_all | solution.py:675
  26.2 2.0 %inner.1 = bf16[3,16,16,128]{3,2,1,0:T(8,128)(2,1)} custom-call(f32[16,2,128]{2,1,0:T(2,128)S(1)} %all-to-all-done.1.arrived, f32[8,128]{1,0:T(8,128)S(1)} %get-tuple-element.25.stats, f32[3,256,128]{2,1,0:T(8,128)S(1)} %get-tuple-element.26.direct, bf16[3,16,16,128]{3,2,1,0:T(8,128)(2,1)S(1)} %get-tuple-element.20.hidden, ...), custom_call_target="tpu_custom_call" | custom-call | tf_op jit(solution)/shard_map/inner/pallas_call | solution.py:689
Async XLA Ops:
  4.5 11.3 %all-to-all-start = ((f32[16,4,128]{2,1,0:T(4,128)}), f32[16,4,128]{2,1,0:T(4,128)S(1)}, u32[]{:S(2)}, u32[]{:S(2)}) async-start(f32[16,4,128]{2,1,0:T(4,128)} %get-tuple-element.19), calls=%async_computation | async-start | bytes 65536 | tf_op jit(solution)/shard_map/all_to_all | solution.py:656
  12.4 11.5 %collective-permute-start = (bf16[1,16,16,128]{3,2,1,0:T(8,128)(2,1)S(1)}, bf16[1,16,16,128]{3,2,1,0:T(8,128)(2,1)S(1)}, u32[]{:S(2)}, u32[]{:S(2)}) collective-permute-start(bf16[1,16,16,128]{3,2,1,0:T(8,128)(2,1)S(1)} %get-tuple-element.27), channel_id=1, source_target_pairs={{0,1},{2,3},{4,5},{6,7},{8,9},{10,11},{12,13},{14,15},{1,0},{3,2},... | collective-permute-start | bytes 196616 | tf_op jit(solution)/shard_map/ppermute | solution.py:672
  12.5 11.4 %collective-permute-start.1 = (bf16[1,16,16,128]{3,2,1,0:T(8,128)(2,1)S(1)}, bf16[1,16,16,128]{3,2,1,0:T(8,128)(2,1)S(1)}, u32[]{:S(2)}, u32[]{:S(2)}) collective-permute-start(bf16[1,16,16,128]{3,2,1,0:T(8,128)(2,1)S(1)} %get-tuple-element.28), channel_id=1, source_target_pairs={{1,2},{3,4},{5,6},{7,8},{9,10},{11,12},{13,14},{2,1},{4,3},{6,5},{... | collective-permute-start | bytes 196616 | tf_op jit(solution)/shard_map/ppermute | solution.py:674
  17.5 8.7 %all-to-all-start.1 = ((f32[16,2,128]{2,1,0:T(2,128)}), f32[16,2,128]{2,1,0:T(2,128)S(1)}, u32[]{:S(2)}, u32[]{:S(2)}) async-start(f32[16,2,128]{2,1,0:T(2,128)} %get-tuple-element.24), calls=%async_computation.1 | async-start | bytes 32768 | tf_op jit(solution)/shard_map/all_to_all | solution.py:675

commit v9 on v8

--- a/solution.py
+++ b/solution.py
@@ -119,7 +119,7 @@
 
 
 def first_order(devices):
-    return led_by(devices * 13 // 16, devices)
+    return led_by(devices * 11 // 16, devices)
 
 
 def message_shape(devices):

time: 28.5 us -> 28.4 us (level)
  no operation moved by 1% of the time
where the time goes in v9:
time: 28.4 us; the launch traced here: 28.1 us
  starting transfers between devices  14.9 us (52%)
  Pallas kernels  9.78 us (34%)
  waiting for transfers between devices  3.4 us (12%)
    all_to_all x1, starting transfers between devices, per_device(): lax.all_to_all(send, 'row', 0, 0, axis_index_groups=[first_order(devices)...  7.82 us
    all_to_all x1, starting transfers between devices, per_device(): lax.all_to_all(sums, 'row', 0, 0, axis_index_groups=[led_by(devices - 1,...  6.29 us
    pallas_call x1, Pallas kernels, per_device(): pl.pallas_call(reward_kernel, out_shape=message + tuple((pltpu.VMEM(x.sha...  4.46 us
    all_to_all x1, waiting for transfers between devices, per_device(): lax.all_to_all(send, 'row', 0, 0, axis_index_groups=[first_order(devices)...  2.53 us
    pallas_call x1, Pallas kernels, per_device(): pl.pallas_call(functools.partial(inner_kernel, devices=devices), out_shap...  1.96 us
    pallas_call x1, Pallas kernels, per_device(): pl.pallas_call(slope_kernel, out_shape=slope_outs, in_specs=[VMEM] * 5 +...  1.71 us
    pallas_call x1, Pallas kernels, per_device(): pl.pallas_call(late_kernel, out_shape=(pltpu.VMEM((2, cells, channels), F...  1.47 us
    all_to_all x1, waiting for transfers between devices, per_device(): lax.all_to_all(sums, 'row', 0, 0, axis_index_groups=[led_by(devices - 1,...  0.87 us
  transfers between devices with their start and end apart: 4, of which 2 were waited for; matrix products, arithmetic and copies ran while one was open for 0% of the time, Pallas kernels for 12%

profile of v9, /device:TPU:0, one launch (start us, length us, event | category | flops | bytes accessed | tf_op | source)
XLA Modules:
  0.0 28.1 jit_solution(8895162091885902071)
XLA Ops:
  0.0 4.5 %reward.1 = (f32[16,4,128]{2,1,0:T(4,128)}, bf16[1,16,16,128]{3,2,1,0:T(8,128)(2,1)S(1)}, bf16[1,16,16,128]{3,2,1,0:T(8,128)(2,1)S(1)}, bf16[3,16,16,128]{3,2,1,...) custom-call(bf16[3,16,48]{2,1,0:T(8,128)(2,1)} %bitcast.7, ...), custom_call_target="tpu_custom_call" | custom-call | tf_op jit(solution)/shard_map/reward/pallas_call | solution.py:604
  4.5 7.8 %all-to-all-start = ((f32[16,4,128]{2,1,0:T(4,128)}), f32[16,4,128]{2,1,0:T(4,128)S(1)}, u32[]{:S(2)}, u32[]{:S(2)}) async-start(f32[16,4,128]{2,1,0:T(4,128)} %get-tuple-element.19), calls=%async_computation | async-start | bytes 65536 | tf_op jit(solution)/shard_map/all_to_all | solution.py:656
  12.3 0.1 collective-permute-start
  12.4 0.7 %collective-permute-start.1 = (bf16[1,16,16,128]{3,2,1,0:T(8,128)(2,1)S(1)}, bf16[1,16,16,128]{3,2,1,0:T(8,128)(2,1)S(1)}, u32[]{:S(2)}, u32[]{:S(2)}) collective-permute-start(bf16[1,16,16,128]{3,2,1,0:T(8,128)(2,1)S(1)} %get-tuple-element.28), channel_id=1, source_target_pairs={{1,2},{3,4},{5,6},{7,8},{9,10},{11,12},{13,14},{2,1},{4,3},{6,5},{... | collective-permute-start | bytes 196616 | tf_op jit(solution)/shard_map/ppermute | solution.py:674
  13.0 0.2 prepare.1.wide
  13.2 2.5 %all-to-all-done.arrived = f32[16,4,128]{2,1,0:T(4,128)S(1)} async-done(((f32[16,4,128]{2,1,0:T(4,128)}), f32[16,4,128]{2,1,0:T(4,128)S(1)}, u32[]{:S(2)}, u32[]{:S(2)}) %all-to-all-start) | async-done | bytes 32800 | tf_op jit(solution)/shard_map/all_to_all | solution.py:656
  15.8 1.7 %slope.1 = (f32[3,256,128]{2,1,0:T(8,128)S(1)}, f32[2,256,128]{2,1,0:T(8,128)S(1)}, f32[8,128]{1,0:T(8,128)S(1)}, f32[16,2,128]{2,1,0:T(2,128)}) custom-call(f32[16,4,128]{2,1,0:T(4,128)S(1)} %all-to-all-done.arrived, bf16[3,16,16,128]{3,2,1,0:T(8,128)(2,1)S(1)} %get-tuple-element.20.hidden, f32[1,128]{1,0:T(1,128)S(1)} %get-tuple-element.21.gain, ...), custom_call_target="tpu_custom_call" | custom-call | tf_op jit(solution)/shard_map/slope/pallas_call | solution.py:657
  17.5 6.3 %all-to-all-start.1 = ((f32[16,2,128]{2,1,0:T(2,128)}), f32[16,2,128]{2,1,0:T(2,128)S(1)}, u32[]{:S(2)}, u32[]{:S(2)}) async-start(f32[16,2,128]{2,1,0:T(2,128)} %get-tuple-element.24), calls=%async_computation.1 | async-start | bytes 32768 | tf_op jit(solution)/shard_map/all_to_all | solution.py:675
  23.8 0.0 collective-permute-done.across
  23.8 0.0 collective-permute-done.1.along
  23.8 1.5 %late.1 = (f32[2,256,128]{2,1,0:T(8,128)S(1)}, bf16[2,16,16,128]{3,2,1,0:T(8,128)(2,1)S(1)}, bf16[1152,384]{1,0:T(8,128)(2,1)S(1)}) custom-call(bf16[1,16,16,128]{3,2,1,0:T(8,128)(2,1)S(1)} %collective-permute-done.across, bf16[1,16,16,128]{3,2,1,0:T(8,128)(2,1)S(1)} %collective-permute-done.1.along, ...), custom_call_target="tpu_custom_call", output_to_operand_aliasing={{0}: (2, {})} | custom-call | tf_op jit(solution)/shard_map/late/pallas_call | solution.py:676
  25.3 0.9 %all-to-all-done.1.arrived = f32[16,2,128]{2,1,0:T(2,128)S(1)} async-done(((f32[16,2,128]{2,1,0:T(2,128)}), f32[16,2,128]{2,1,0:T(2,128)S(1)}, u32[]{:S(2)}, u32[]{:S(2)}) %all-to-all-start.1) | async-done | bytes 16416 | tf_op jit(solution)/shard_map/all_to_all | solution.py:675
  26.1 2.0 %inner.1 = bf16[3,16,16,128]{3,2,1,0:T(8,128)(2,1)} custom-call(f32[16,2,128]{2,1,0:T(2,128)S(1)} %all-to-all-done.1.arrived, f32[8,128]{1,0:T(8,128)S(1)} %get-tuple-element.25.stats, f32[3,256,128]{2,1,0:T(8,128)S(1)} %get-tuple-element.26.direct, bf16[3,16,16,128]{3,2,1,0:T(8,128)(2,1)S(1)} %get-tuple-element.20.hidden, ...), custom_call_target="tpu_custom_call" | custom-call | tf_op jit(solution)/shard_map/inner/pallas_call | solution.py:689
Async XLA Ops:
  4.5 11.3 %all-to-all-start = ((f32[16,4,128]{2,1,0:T(4,128)}), f32[16,4,128]{2,1,0:T(4,128)S(1)}, u32[]{:S(2)}, u32[]{:S(2)}) async-start(f32[16,4,128]{2,1,0:T(4,128)} %get-tuple-element.19), calls=%async_computation | async-start | bytes 65536 | tf_op jit(solution)/shard_map/all_to_all | solution.py:656
  12.3 11.5 %collective-permute-start = (bf16[1,16,16,128]{3,2,1,0:T(8,128)(2,1)S(1)}, bf16[1,16,16,128]{3,2,1,0:T(8,128)(2,1)S(1)}, u32[]{:S(2)}, u32[]{:S(2)}) collective-permute-start(bf16[1,16,16,128]{3,2,1,0:T(8,128)(2,1)S(1)} %get-tuple-element.27), channel_id=1, source_target_pairs={{0,1},{2,3},{4,5},{6,7},{8,9},{10,11},{12,13},{14,15},{1,0},{3,2},... | collective-permute-start | bytes 196616 | tf_op jit(solution)/shard_map/ppermute | solution.py:672
  12.4 11.4 %collective-permute-start.1 = (bf16[1,16,16,128]{3,2,1,0:T(8,128)(2,1)S(1)}, bf16[1,16,16,128]{3,2,1,0:T(8,128)(2,1)S(1)}, u32[]{:S(2)}, u32[]{:S(2)}) collective-permute-start(bf16[1,16,16,128]{3,2,1,0:T(8,128)(2,1)S(1)} %get-tuple-element.28), channel_id=1, source_target_pairs={{1,2},{3,4},{5,6},{7,8},{9,10},{11,12},{13,14},{2,1},{4,3},{6,5},{... | collective-permute-start | bytes 196616 | tf_op jit(solution)/shard_map/ppermute | solution.py:674
  17.5 8.7 %all-to-all-start.1 = ((f32[16,2,128]{2,1,0:T(2,128)}), f32[16,2,128]{2,1,0:T(2,128)S(1)}, u32[]{:S(2)}, u32[]{:S(2)}) async-start(f32[16,2,128]{2,1,0:T(2,128)} %get-tuple-element.24), calls=%async_computation.1 | async-start | bytes 32768 | tf_op jit(solution)/shard_map/all_to_all | solution.py:675

commit v10 on v9

--- a/solution.py
+++ b/solution.py
@@ -672,7 +672,7 @@
     across = lax.ppermute(across, "row", swaps + [(b, a) for a, b in swaps])
     swaps = [(2 * i - 1, 2 * i) for i in range(1, devices // 2)]
     along = lax.ppermute(along, "row", swaps + [(b, a) for a, b in swaps])
-    summed = lax.all_to_all(sums, "row", 0, 0, axis_index_groups=[led_by(devices - 1, devices)], tiled=True)
+    summed = lax.all_to_all(sums, "row", 0, 0, axis_index_groups=[first_order(devices)], tiled=True)
     edge_direct, edge_states, turned = pl.pallas_call(
         late_kernel,
         out_shape=(

time: 28.4 us -> 28.3 us (level)
  starting transfers between devices: 14.9 us -> 13.8 us
  waiting for transfers between devices: 3.4 us -> 4.29 us
    all_to_all x1, starting transfers between devices: 6.29 us -> 5.28 us  [per_device(): lax.all_to_all(sums, 'row', 0, 0, axis_index_groups=[first_order(devices)...]
    all_to_all x1, waiting for transfers between devices: 0.87 us -> 1.75 us  [per_device(): lax.all_to_all(sums, 'row', 0, 0, axis_index_groups=[first_order(devices)...]
where the time goes in v10:
time: 28.3 us; the launch traced here: 28 us
  starting transfers between devices  13.8 us (49%)
  Pallas kernels  9.78 us (35%)
  waiting for transfers between devices  4.29 us (15%)
    all_to_all x1, starting transfers between devices, per_device(): lax.all_to_all(send, 'row', 0, 0, axis_index_groups=[first_order(devices)...  7.82 us
    all_to_all x1, starting transfers between devices, per_device(): lax.all_to_all(sums, 'row', 0, 0, axis_index_groups=[first_order(devices)...  5.28 us
    pallas_call x1, Pallas kernels, per_device(): pl.pallas_call(reward_kernel, out_shape=message + tuple((pltpu.VMEM(x.sha...  4.46 us
    all_to_all x1, waiting for transfers between devices, per_device(): lax.all_to_all(send, 'row', 0, 0, axis_index_groups=[first_order(devices)...  2.53 us
    pallas_call x1, Pallas kernels, per_device(): pl.pallas_call(functools.partial(inner_kernel, devices=devices), out_shap...  1.96 us
    all_to_all x1, waiting for transfers between devices, per_device(): lax.all_to_all(sums, 'row', 0, 0, axis_index_groups=[first_order(devices)...  1.75 us
    pallas_call x1, Pallas kernels, per_device(): pl.pallas_call(slope_kernel, out_shape=slope_outs, in_specs=[VMEM] * 5 +...  1.71 us
    pallas_call x1, Pallas kernels, per_device(): pl.pallas_call(late_kernel, out_shape=(pltpu.VMEM((2, cells, channels), F...  1.47 us
  transfers between devices with their start and end apart: 4, of which 2 were waited for; matrix products, arithmetic and copies ran while one was open for 0% of the time, Pallas kernels for 12%

profile of v10, /device:TPU:0, one launch (start us, length us, event | category | flops | bytes accessed | tf_op | source)
XLA Modules:
  0.0 28.0 jit_solution(7413449702384740929)
XLA Ops:
  0.0 4.5 %reward.1 = (f32[16,4,128]{2,1,0:T(4,128)}, bf16[1,16,16,128]{3,2,1,0:T(8,128)(2,1)S(1)}, bf16[1,16,16,128]{3,2,1,0:T(8,128)(2,1)S(1)}, bf16[3,16,16,128]{3,2,1,...) custom-call(bf16[3,16,48]{2,1,0:T(8,128)(2,1)} %bitcast.7, ...), custom_call_target="tpu_custom_call" | custom-call | tf_op jit(solution)/shard_map/reward/pallas_call | solution.py:604
  4.5 7.8 %all-to-all-start = ((f32[16,4,128]{2,1,0:T(4,128)}), f32[16,4,128]{2,1,0:T(4,128)S(1)}, u32[]{:S(2)}, u32[]{:S(2)}) async-start(f32[16,4,128]{2,1,0:T(4,128)} %get-tuple-element.19), calls=%async_computation | async-start | bytes 65536 | tf_op jit(solution)/shard_map/all_to_all | solution.py:656
  12.3 0.1 collective-permute-start
  12.4 0.7 %collective-permute-start.1 = (bf16[1,16,16,128]{3,2,1,0:T(8,128)(2,1)S(1)}, bf16[1,16,16,128]{3,2,1,0:T(8,128)(2,1)S(1)}, u32[]{:S(2)}, u32[]{:S(2)}) collective-permute-start(bf16[1,16,16,128]{3,2,1,0:T(8,128)(2,1)S(1)} %get-tuple-element.28), channel_id=1, source_target_pairs={{1,2},{3,4},{5,6},{7,8},{9,10},{11,12},{13,14},{2,1},{4,3},{6,5},{... | collective-permute-start | bytes 196616 | tf_op jit(solution)/shard_map/ppermute | solution.py:674
  13.0 0.2 prepare.1.wide
  13.2 2.5 %all-to-all-done.arrived = f32[16,4,128]{2,1,0:T(4,128)S(1)} async-done(((f32[16,4,128]{2,1,0:T(4,128)}), f32[16,4,128]{2,1,0:T(4,128)S(1)}, u32[]{:S(2)}, u32[]{:S(2)}) %all-to-all-start) | async-done | bytes 32800 | tf_op jit(solution)/shard_map/all_to_all | solution.py:656
  15.8 1.7 %slope.1 = (f32[3,256,128]{2,1,0:T(8,128)S(1)}, f32[2,256,128]{2,1,0:T(8,128)S(1)}, f32[8,128]{1,0:T(8,128)S(1)}, f32[16,2,128]{2,1,0:T(2,128)}) custom-call(f32[16,4,128]{2,1,0:T(4,128)S(1)} %all-to-all-done.arrived, bf16[3,16,16,128]{3,2,1,0:T(8,128)(2,1)S(1)} %get-tuple-element.20.hidden, f32[1,128]{1,0:T(1,128)S(1)} %get-tuple-element.21.gain, ...), custom_call_target="tpu_custom_call" | custom-call | tf_op jit(solution)/shard_map/slope/pallas_call | solution.py:657
  17.5 5.3 %all-to-all-start.1 = ((f32[16,2,128]{2,1,0:T(2,128)}), f32[16,2,128]{2,1,0:T(2,128)S(1)}, u32[]{:S(2)}, u32[]{:S(2)}) async-start(f32[16,2,128]{2,1,0:T(2,128)} %get-tuple-element.24), calls=%async_computation.1 | async-start | bytes 32768 | tf_op jit(solution)/shard_map/all_to_all | solution.py:675
  22.8 0.0 collective-permute-done.across
  22.8 0.0 collective-permute-done.1.along
  22.8 1.5 %late.1 = (f32[2,256,128]{2,1,0:T(8,128)S(1)}, bf16[2,16,16,128]{3,2,1,0:T(8,128)(2,1)S(1)}, bf16[1152,384]{1,0:T(8,128)(2,1)S(1)}) custom-call(bf16[1,16,16,128]{3,2,1,0:T(8,128)(2,1)S(1)} %collective-permute-done.across, bf16[1,16,16,128]{3,2,1,0:T(8,128)(2,1)S(1)} %collective-permute-done.1.along, ...), custom_call_target="tpu_custom_call", output_to_operand_aliasing={{0}: (2, {})} | custom-call | tf_op jit(solution)/shard_map/late/pallas_call | solution.py:676
  24.2 1.7 %all-to-all-done.1.arrived = f32[16,2,128]{2,1,0:T(2,128)S(1)} async-done(((f32[16,2,128]{2,1,0:T(2,128)}), f32[16,2,128]{2,1,0:T(2,128)S(1)}, u32[]{:S(2)}, u32[]{:S(2)}) %all-to-all-start.1) | async-done | bytes 16416 | tf_op jit(solution)/shard_map/all_to_all | solution.py:675
  26.0 2.0 %inner.1 = bf16[3,16,16,128]{3,2,1,0:T(8,128)(2,1)} custom-call(f32[16,2,128]{2,1,0:T(2,128)S(1)} %all-to-all-done.1.arrived, f32[8,128]{1,0:T(8,128)S(1)} %get-tuple-element.25.stats, f32[3,256,128]{2,1,0:T(8,128)S(1)} %get-tuple-element.26.direct, bf16[3,16,16,128]{3,2,1,0:T(8,128)(2,1)S(1)} %get-tuple-element.20.hidden, ...), custom_call_target="tpu_custom_call" | custom-call | tf_op jit(solution)/shard_map/inner/pallas_call | solution.py:689
Async XLA Ops:
  4.5 11.3 %all-to-all-start = ((f32[16,4,128]{2,1,0:T(4,128)}), f32[16,4,128]{2,1,0:T(4,128)S(1)}, u32[]{:S(2)}, u32[]{:S(2)}) async-start(f32[16,4,128]{2,1,0:T(4,128)} %get-tuple-element.19), calls=%async_computation | async-start | bytes 65536 | tf_op jit(solution)/shard_map/all_to_all | solution.py:656
  12.3 10.5 %collective-permute-start = (bf16[1,16,16,128]{3,2,1,0:T(8,128)(2,1)S(1)}, bf16[1,16,16,128]{3,2,1,0:T(8,128)(2,1)S(1)}, u32[]{:S(2)}, u32[]{:S(2)}) collective-permute-start(bf16[1,16,16,128]{3,2,1,0:T(8,128)(2,1)S(1)} %get-tuple-element.27), channel_id=1, source_target_pairs={{0,1},{2,3},{4,5},{6,7},{8,9},{10,11},{12,13},{14,15},{1,0},{3,2},... | collective-permute-start | bytes 196616 | tf_op jit(solution)/shard_map/ppermute | solution.py:672
  12.4 10.4 %collective-permute-start.1 = (bf16[1,16,16,128]{3,2,1,0:T(8,128)(2,1)S(1)}, bf16[1,16,16,128]{3,2,1,0:T(8,128)(2,1)S(1)}, u32[]{:S(2)}, u32[]{:S(2)}) collective-permute-start(bf16[1,16,16,128]{3,2,1,0:T(8,128)(2,1)S(1)} %get-tuple-element.28), channel_id=1, source_target_pairs={{1,2},{3,4},{5,6},{7,8},{9,10},{11,12},{13,14},{2,1},{4,3},{6,5},{... | collective-permute-start | bytes 196616 | tf_op jit(solution)/shard_map/ppermute | solution.py:674
  17.5 8.5 %all-to-all-start.1 = ((f32[16,2,128]{2,1,0:T(2,128)}), f32[16,2,128]{2,1,0:T(2,128)S(1)}, u32[]{:S(2)}, u32[]{:S(2)}) async-start(f32[16,2,128]{2,1,0:T(2,128)} %get-tuple-element.24), calls=%async_computation.1 | async-start | bytes 32768 | tf_op jit(solution)/shard_map/all_to_all | solution.py:675
